TPU v7x, 128 devices: a whole 4x4x4 slice. The times are simulated.
128 devices in a mesh: space: 32 (over x, z, core), rep: 4 (over y).
Axes of the slice: x: 4, y: 4, z: 4, core: 2. Of those that a mesh axis runs over, the one named last changes fastest.
Arguments:
- features: bfloat16 [4, 32768, 256], P('rep', 'space'), may hold values from -36 to 36
- neighbours: int32 [4, 64, 26], P('rep', 'space'), may hold values from -1 to 63, as said below
- serial_order: int32 [4, 32768], P('rep', 'space'), may hold values from 0 to 32767, as said below
- kernel_weight: bfloat16 [27, 256, 256], replicated, may hold values from -0.078125 to 0.078125
- input_projection: bfloat16 [256, 768], replicated, may hold values from -2.4 to 2.4
- output_projection: bfloat16 [256, 256], replicated, may hold values from -1.5 to 1.5
- cotangent: bfloat16 [4, 32768, 256], P('rep', 'space'), may hold values from -0.625 to 0.625
Outputs:
- encoded: bfloat16 [4, 32768, 256], P('rep', 'space')
- attended: bfloat16 [4, 32768, 256], P('rep', 'space')
- projection_gradient: float32 [256, 256], replicated
Inputs may be any that keep to these rules, and one draw needn't show every extreme that they name: neighbours[t, b, n] is the brick of tile t beside brick b at the n-th offset, or -1; brick b lies on index b // 2 of space, and every brick beside it lies on the same index or the one just before or just after; those on the index before are at offsets with p = -1, those after at p = 1. If c is beside b at an offset, b is beside c at the opposite offset. serial_order[t] is a permutation of 0 to 32767; a point goes to index serial_order[t, r] // 1024 of space. One index of space sends at most 48 points to any one index, exactly 48 to some, and every index sends the same number of points to the index k places further along space (counted modulo the axis) for each k.
All inputs are finite; a program needn't handle non-finite values.
Results may differ from a plain program's by a relative error of at most 0.009.
The roundings to bfloat16 on the way count: a program that leaves them out, or rounds other values in their place, can miss the bound.
Values may be sent and summed in bfloat16 or wider, within the bound.
A program may use at most 128 MiB of HBM per device.

v0:
```python
import functools

import jax
import jax.numpy as jnp
from jax import lax
from jax.experimental import pallas as pl
from jax.experimental.pallas import tpu as pltpu
from jax.sharding import PartitionSpec as P

HEADS = 16
EDGE = 8
MESH = pl.DeviceIdType.MESH
F32 = jnp.float32
BF16 = jnp.bfloat16
VMEM_LIMIT = 60 * 1024 * 1024


def dot(a, b):
    return jnp.dot(a, b, preferred_element_type=F32)


def dot_t(a, b):
    return lax.dot_general(a, b, (((1,), (1,)), ((), ())), preferred_element_type=F32)


def iota(shape, dim):
    return lax.broadcasted_iota(jnp.int32, shape, dim)


def onehot(mask):
    return jnp.where(mask, 1.0, 0.0).astype(BF16)


def front_kernel(
    spaces, cap, feat, nb, order, w_hbm, enc, reg,
    w, x, halo_l, halo_r, table, got, send, recv,
    w_sem, hs, hr, ts, tr, rs, rr,
):
    me = lax.axis_index("space")
    rows, width = feat.shape
    face = EDGE * EDGE
    brick = EDGE * face
    bricks = rows // brick
    load = pltpu.make_async_copy(w_hbm, w, w_sem)
    load.start()

    def peer(k):
        return {"space": lax.rem(me + k, spaces)}

    barrier = pltpu.get_barrier_semaphore()

    def greet(k, carry):
        pl.semaphore_signal(barrier, inc=1, device_id=peer(k), device_id_type=MESH)
        return carry

    lax.fori_loop(1, spaces, greet, 0)

    places = order[...]
    shift = rows.bit_length() - 1
    owner = lax.shift_right_logical(places, shift)
    slot = places & (rows - 1)
    ahead = (owner - me + spaces) & (spaces - 1)
    chosen = jnp.where(iota((spaces, rows), 0) == ahead, 1.0, 0.0)
    before = onehot(iota((rows, rows), 0) < iota((rows, rows), 1))
    rank = jnp.sum(chosen * dot(chosen.astype(BF16), before), axis=0, keepdims=True)
    high = lax.shift_right_logical(slot, 5).astype(F32)
    low = (slot & 31).astype(F32)
    lanes = table.shape[2]
    by_rank = onehot(iota((lanes, rows), 0).astype(F32) == rank)
    stacked = jnp.concatenate([chosen * high, chosen * low, chosen], axis=0).astype(BF16)
    found = dot_t(stacked, by_rank)
    slots = found[:spaces] * 32.0 + found[spaces : 2 * spaces]
    slots = jnp.where(found[2 * spaces :] > 0.5, slots, -1.0)
    table[...] = jnp.broadcast_to(slots[:, None, :], table.shape)
    row_at = ahead.astype(F32) * float(cap) + rank

    pl.semaphore_wait(barrier, spaces - 1)

    halos = []
    for b in range(bricks):
        for source, dst, step, n in (
            (b * brick + brick - face, halo_l, 1, 2 * b),
            (b * brick, halo_r, spaces - 1, 2 * b + 1),
        ):
            copy = pltpu.make_async_remote_copy(
                src_ref=feat.at[pl.ds(source, face)], dst_ref=dst.at[b], send_sem=hs.at[n], recv_sem=hr.at[n],
                device_id=peer(step), device_id_type=MESH,
            )
            copy.start()
            halos.append(copy)

    def table_copy(k):
        return pltpu.make_async_remote_copy(
            src_ref=table.at[k], dst_ref=got.at[k], send_sem=ts.at[k], recv_sem=tr.at[k],
            device_id=peer(k), device_id_type=MESH,
        )

    def row_copy(k):
        return pltpu.make_async_remote_copy(
            src_ref=send.at[k], dst_ref=recv.at[k], send_sem=rs.at[k], recv_sem=rr.at[k],
            device_id=peer(k), device_id_type=MESH,
        )

    def start_table(k, carry):
        table_copy(k).start()
        return carry

    lax.fori_loop(1, spaces, start_table, 0)

    depth = iota((EDGE + 2, EDGE, width), 1)

    def beside(b, offset, source_id):
        p, q, r = offset
        number = 9 * (p + 1) + 3 * (q + 1) + (r + 1)
        number -= number > 13
        target = nb[b, number]
        return jnp.where((target == source_id) & (target >= 0), 1.0, 0.0)

    def layer(ref, first):
        return ref[pl.ds(first, face)].astype(F32).reshape(EDGE, EDGE, width)

    def write_layer(b, i, p, sources, ids, own):
        grown = []
        for r in (-1, 0, 1):
            parts = []
            for q in (-1, 0, 1):
                part = slice(EDGE - 1, EDGE) if q < 0 else slice(0, 1) if q > 0 else slice(0, EDGE)
                if own is not None and q == 0 and r == 0:
                    parts.append(own)
                    continue
                total = None
                for source, one_id in zip(sources, ids):
                    term = source[part] * beside(b, (p, q, r), one_id)
                    total = term if total is None else total + term
                parts.append(total)
            grown.append(jnp.concatenate(parts, axis=0))
        below, here, above = grown
        variants = (
            pltpu.roll(jnp.where(depth == EDGE - 1, below, here), 1, 1),
            here,
            pltpu.roll(jnp.where(depth == 0, above, here), EDGE - 1, 1),
        )
        first = i * face if isinstance(i, int) else pl.multiple_of(i * face, face)
        for q in range(3):
            for r in range(3):
                n = 3 * q + r
                x[b, pl.ds(first, face), n * width : (n + 1) * width] = (
                    variants[r][q : q + EDGE].reshape(face, width).astype(BF16)
                )

    own_ids = [me * bricks + n for n in range(bricks)]
    left_ids = [(me - 1) * bricks + n for n in range(bricks)]
    right_ids = [(me + 1) * bricks + n for n in range(bricks)]

    def inner(i, carry):
        sources = [layer(feat, pl.multiple_of(n * brick + i * face, face)) for n in range(bricks)]
        for b in range(bricks):
            write_layer(b, i + 1, 0, sources, own_ids, sources[b])
        return carry

    lax.fori_loop(0, EDGE, inner, 0)

    for copy in halos:
        copy.wait_recv()
    tops = [layer(feat, n * brick + brick - face) for n in range(bricks)]
    bottoms = [layer(feat, n * brick) for n in range(bricks)]
    lefts = [layer(halo_l.at[n], 0) for n in range(bricks)]
    rights = [layer(halo_r.at[n], 0) for n in range(bricks)]
    for b in range(bricks):
        write_layer(b, 0, -1, lefts + tops, left_ids + own_ids, None)
        write_layer(b, EDGE + 1, 1, bottoms + rights, own_ids + right_ids, None)

    load.wait()
    tile = 256

    def conv(n, carry):
        b, first = n // (brick // tile), n % (brick // tile) * tile
        acc = jnp.zeros((tile, width), F32)
        for p in range(3):
            window = x[b, pl.ds(pl.multiple_of(first + p * face, face), tile), :]
            acc = acc + dot(window, w[9 * p : 9 * p + 9].reshape(9 * width, width))
        at = pl.ds(pl.multiple_of(n * tile, tile), tile)
        enc[at] = (feat[at].astype(F32) + acc).astype(BF16)
        return carry

    lax.fori_loop(0, rows // tile, conv, 0)

    group = 8
    for c in range(spaces // group):
        wanted = (iota((group * cap, rows), 0) + c * group * cap).astype(F32)
        block = dot(onehot(wanted == row_at), enc[...]).astype(BF16)
        send[c * group : (c + 1) * group] = block.reshape(group, cap, width)
        for k in range(max(1, c * group), (c + 1) * group):
            row_copy(k).start()
    recv[0] = send[0]
    got[0] = table[0]

    def wait_table(k, carry):
        table_copy(k).wait()
        return carry

    lax.fori_loop(1, spaces, wait_table, 0)
    total = jnp.zeros((rows, width), F32)
    column = iota((8, 128), 1)
    for c in range(spaces // group):
        for k in range(max(1, c * group), (c + 1) * group):
            row_copy(k).wait_recv()
        blocks = []
        for t in range(c * group * cap // 128, (c + 1) * group * cap // 128):
            lane = jnp.full((8, 128), -1.0, F32)
            for k in range(spaces):
                start, end = max(0, k * cap - 128 * t), min(128, (k + 1) * cap - 128 * t)
                if start >= end:
                    continue
                moved = got[k]
                if (k * cap - 128 * t) % 128:
                    moved = pltpu.roll(moved, (k * cap - 128 * t) % 128, 1)
                lane = jnp.where((column >= start) & (column < end), moved, lane)
            blocks.append(onehot(iota((rows, 128), 0).astype(F32) == lane[0:1]))
        arrived = recv[c * group : (c + 1) * group].reshape(group * cap, width)
        total = total + dot(jnp.concatenate(blocks, axis=1), arrived)
    reg[...] = total.astype(BF16)

    def wait_sent(k, carry):
        row_copy(k).wait_send()
        return carry

    lax.fori_loop(1, spaces, wait_sent, 0)
    for copy in halos:
        copy.wait_send()


def front(features, neighbours, order, weight):
    spaces = lax.axis_size("space")
    rows, width = features.shape
    cap = 3 * rows // (2 * spaces)
    bricks = rows // EDGE**3
    face = EDGE * EDGE
    vmem = pl.BlockSpec(memory_space=pltpu.VMEM)
    return pl.pallas_call(
        functools.partial(front_kernel, spaces, cap),
        out_shape=[jax.ShapeDtypeStruct((rows, width), BF16)] * 2,
        in_specs=[vmem, pl.BlockSpec(memory_space=pltpu.SMEM), vmem, pl.BlockSpec(memory_space=pl.ANY)],
        out_specs=[vmem, vmem],
        scratch_shapes=[
            pltpu.VMEM(weight.shape, BF16),
            pltpu.VMEM((bricks, (EDGE + 2) * face, 9 * width), BF16),
            pltpu.VMEM((bricks, face, width), BF16),
            pltpu.VMEM((bricks, face, width), BF16),
            pltpu.VMEM((spaces, 8, 128), F32),
            pltpu.VMEM((spaces, 8, 128), F32),
            pltpu.VMEM((spaces, cap, width), BF16),
            pltpu.VMEM((spaces, cap, width), BF16),
            pltpu.SemaphoreType.DMA,
            pltpu.SemaphoreType.DMA((2 * bricks,)),
            pltpu.SemaphoreType.DMA((2 * bricks,)),
            pltpu.SemaphoreType.DMA((spaces,)),
            pltpu.SemaphoreType.DMA((spaces,)),
            pltpu.SemaphoreType.DMA((spaces,)),
            pltpu.SemaphoreType.DMA((spaces,)),
        ],
        compiler_params=pltpu.CompilerParams(collective_id=0, has_side_effects=True, vmem_limit_bytes=VMEM_LIMIT),
        cost_estimate=pl.CostEstimate(
            flops=2 * rows * 27 * width * width, bytes_accessed=weight.size * 2 + 6 * rows * width, transcendentals=0
        ),
        name="front",
    )(features, neighbours, order, weight)


def attention_kernel(reg, wi, wo, cot, att, grad, q, k, v, ctx):
    rows, width = reg.shape
    head = width // HEADS
    half = width // 2
    residual = reg[...].astype(F32)
    centred = residual - jnp.mean(residual, axis=-1, keepdims=True)
    variance = jnp.mean(centred * centred, axis=-1, keepdims=True)
    normed = (centred * lax.rsqrt(variance + 1e-05)).astype(BF16)
    packed = dot(normed, wi[...]).astype(BF16)
    q[...] = packed[:, :width] * jnp.asarray(head**-0.5, BF16)
    k[...] = packed[:, width : 2 * width]
    ones = jnp.ones((rows, half), BF16)
    for n in range(2):
        v[n] = jnp.concatenate([packed[:, 2 * width + n * half : 2 * width + (n + 1) * half], ones], axis=1)
    ctx[...] = jnp.zeros_like(ctx)
    tile = 256
    lane_q = iota((tile, width), 1) // head
    lane_c = iota((tile, half), 1) // head

    def one_head(h, carry):
        side = h // (HEADS // 2)
        values = v[side]
        for t in range(rows // tile):
            at = slice(t * tile, (t + 1) * tile)
            queries = jnp.where(lane_q == h, q[at], jnp.zeros((), BF16))
            scores = dot_t(queries, k[...])
            lifted = jnp.exp(scores - jnp.max(scores, axis=-1, keepdims=True))
            both = dot(lifted.astype(BF16), values)
            ratio = both[:, :half] / both[:, half:]
            ctx[side, at] += jnp.where(lane_c == h - side * (HEADS // 2), ratio, 0.0)
        return carry

    lax.fori_loop(0, HEADS, one_head, 0)
    context = jnp.concatenate([ctx[0], ctx[1]], axis=1).astype(BF16)
    att[...] = (residual + dot(context, wo[...])).astype(BF16)
    grad[...] = lax.dot_general(context, cot[...], (((0,), (0,)), ((), ())), preferred_element_type=F32)


def attention(regrouped, wi, wo, cot):
    rows, width = regrouped.shape
    vmem = pl.BlockSpec(memory_space=pltpu.VMEM)
    return pl.pallas_call(
        attention_kernel,
        out_shape=[jax.ShapeDtypeStruct((rows, width), BF16), jax.ShapeDtypeStruct((width, width), F32)],
        in_specs=[vmem] * 4,
        out_specs=[vmem, vmem],
        scratch_shapes=[
            pltpu.VMEM((rows, width), BF16),
            pltpu.VMEM((rows, width), BF16),
            pltpu.VMEM((2, rows, width), BF16),
            pltpu.VMEM((2, rows, width // 2), F32),
        ],
        compiler_params=pltpu.CompilerParams(vmem_limit_bytes=VMEM_LIMIT),
        cost_estimate=pl.CostEstimate(
            flops=4 * HEADS * rows * rows * width, bytes_accessed=8 * rows * width, transcendentals=HEADS * rows * rows
        ),
        name="attention",
    )(regrouped, wi, wo, cot)


def reduce_kernel(spaces, reps, term, out, first, second, part, sum_all, s1, r1, s2, r2, s3, r3, s4, r4):
    space, rep = lax.axis_index("space"), lax.axis_index("rep")
    planes = spaces // 2
    chip, core = space // 2, space % 2
    others = 2 * reps
    place = rep * 2 + core

    def across(n):
        return {"space": lax.rem(chip + n, planes) * 2 + core}

    def along(n):
        there = lax.rem(place + n, others)
        return {"space": chip * 2 + there % 2, "rep": there // 2}

    barrier = pltpu.get_barrier_semaphore()

    def greet_a(n, carry):
        pl.semaphore_signal(barrier, inc=1, device_id=across(n), device_id_type=MESH)
        return carry

    def greet_b(n, carry):
        pl.semaphore_signal(barrier, inc=1, device_id=along(n), device_id_type=MESH)
        return carry

    lax.fori_loop(1, planes, greet_a, 0)
    lax.fori_loop(1, others, greet_b, 0)
    pl.semaphore_wait(barrier, planes + others - 2)

    def copy(src, dst, sems, n, device):
        return pltpu.make_async_remote_copy(
            src_ref=src, dst_ref=dst, send_sem=sems[0].at[n], recv_sem=sems[1].at[n], device_id=device, device_id_type=MESH
        )

    def c1(n):
        there = lax.rem(chip + n, planes)
        return copy(term.at[there], first.at[n], (s1, r1), n, across(n))

    def c2(n):
        there = lax.rem(place + n, others)
        return copy(part.at[there], second.at[n], (s2, r2), n, along(n))

    def c3(n):
        return copy(sum_all.at[chip, place], sum_all.at[chip, place], (s3, r3), n, along(n))

    def w3(n):
        there = lax.rem(place - n + others, others)
        return copy(sum_all.at[chip, there], sum_all.at[chip, there], (s3, r3), n, along(n))

    def c4(n):
        return copy(sum_all.at[chip], sum_all.at[chip], (s4, r4), n, across(n))

    def w4(n):
        there = lax.rem(chip - n + planes, planes)
        return copy(sum_all.at[there], sum_all.at[there], (s4, r4), n, across(n))

    def run(count, make):
        def body(n, carry):
            make(n)
            return carry

        lax.fori_loop(1, count, body, 0)

    run(planes, lambda n: c1(n).start())
    first[0] = term[chip]
    run(planes, lambda n: c1(n).wait())
    part[...] = jnp.sum(first[...], axis=0)
    run(others, lambda n: c2(n).start())
    second[0] = part[place]
    run(others, lambda n: c2(n).wait())
    sum_all[chip, place] = jnp.sum(second[...], axis=0)
    run(others, lambda n: c3(n).start())
    run(others, lambda n: c3(n).wait_send())
    run(others, lambda n: w3(n).wait_recv())
    run(planes, lambda n: c4(n).start())
    run(planes, lambda n: c4(n).wait_send())
    run(planes, lambda n: w4(n).wait_recv())
    out[...] = sum_all[...]


def reduce_all(term):
    spaces, reps = lax.axis_size("space"), lax.axis_size("rep")
    rows, width = term.shape
    planes, others = spaces // 2, 2 * reps
    small = rows // planes // others
    sub = small * width // 128
    shape = (planes, others, sub, 128)
    vmem = pl.BlockSpec(memory_space=pltpu.VMEM)
    out = pl.pallas_call(
        functools.partial(reduce_kernel, spaces, reps),
        out_shape=jax.ShapeDtypeStruct(shape, F32),
        in_specs=[vmem],
        out_specs=vmem,
        scratch_shapes=[
            pltpu.VMEM((planes, others, sub, 128), F32),
            pltpu.VMEM((others, sub, 128), F32),
            pltpu.VMEM((others, sub, 128), F32),
            pltpu.VMEM(shape, F32),
        ]
        + [pltpu.SemaphoreType.DMA((planes,))] * 2
        + [pltpu.SemaphoreType.DMA((others,))] * 4
        + [pltpu.SemaphoreType.DMA((planes,))] * 2,
        compiler_params=pltpu.CompilerParams(collective_id=1, has_side_effects=True),
        name="reduce_all",
    )(term.reshape(shape))
    return out.reshape(rows, width)


def local(features, neighbours, serial_order, kernel_weight, input_projection, output_projection, cotangent):
    encoded, regrouped = front(features[0], neighbours[0], serial_order, kernel_weight)
    attended, term = attention(regrouped, input_projection, output_projection, cotangent[0])
    gradient = reduce_all(term)
    return encoded[None], attended[None], gradient


def solution(mesh):
    in_specs = (
        P("rep", "space", None),
        P("rep", "space", None),
        P("rep", "space"),
        P(),
        P(),
        P(),
        P("rep", "space", None),
    )
    out_specs = (P("rep", "space", None), P("rep", "space", None), P())
    return jax.shard_map(local, mesh=mesh, in_specs=in_specs, out_specs=out_specs, check_vma=False)
```

profile of v0, /device:TPU:1, one launch (start us, length us, event | category | flops | bytes accessed | tf_op | source)
XLA Modules:
  0.0 97.0 jit_solution(18441476039466038327)
XLA Ops:
  0.6 32.8 %front.1 = (bf16[1024,256]{1,0:T(8,128)(2,1)}, bf16[1024,256]{1,0:T(8,128)(2,1)}) custom-call(bf16[1024,256]{1,0:T(8,128)(2,1)} %bitcast.6, s32[2,26]{1,0:T(2,128)} %bitcast.8, s32[1,1024]{1,0:T(1,128)} %order.1, bf16[27,256,256]{2,1,0:T(8,128)(2,1)} %w_hbm.1), custom_call_target="tpu_custom_call" | custom-call | flops 3623878656 | bytes 5111808 | tf_op jit(solution)/shard_map/front/pallas_call | solution.py:240
  33.5 0.0 copy-start
  33.5 31.5 %attention.1 = (bf16[1024,256]{1,0:T(8,128)(2,1)}, f32[256,256]{1,0:T(8,128)}) custom-call(bf16[1024,256]{1,0:T(8,128)(2,1)} %get-tuple-element.8.reg, bf16[256,768]{1,0:T(8,128)(2,1)} %wi.1, bf16[256,256]{1,0:T(8,128)(2,1)} %wo.1, bf16[1024,256]{1,0:T(8,128)(2,1)} %bitcast.7), custom_call_target="tpu_custom_call" | custom-call | flops 17179869184 | bytes 2097152 | tf_op jit(solution)/shard_map/attention/pallas_call | solution.py:311
  65.0 1.8 %reshape.12.term = f32[16,8,4,128]{3,2,1,0:T(4,128)} reshape(f32[256,256]{1,0:T(8,128)} %get-tuple-element.10) | data formatting | bytes 524288 | tf_op jit(solution)/shard_map/reshape | solution.py:433
  66.8 27.7 %reduce_all.1 = f32[16,8,4,128]{3,2,1,0:T(4,128)} custom-call(f32[16,8,4,128]{3,2,1,0:T(4,128)} %reshape.12.term), custom_call_target="tpu_custom_call" | custom-call | tf_op jit(solution)/shard_map/reduce_all/pallas_call | solution.py:417
  94.4 1.8 %reshape.13 = f32[256,256]{1,0:T(8,128)} reshape(f32[16,8,4,128]{3,2,1,0:T(4,128)} %reduce_all.1) | data formatting | bytes 524288 | tf_op jit(solution)/shard_map/reshape | solution.py:434
  96.2 0.0 copy-done
  96.2 0.8 copy.11
Async XLA Ops:
  33.5 62.8 %copy-start = (bf16[1024,256]{1,0:T(8,128)(2,1)S(1)}, bf16[1024,256]{1,0:T(8,128)(2,1)}, u32[]{:S(2)}) copy-start(bf16[1024,256]{1,0:T(8,128)(2,1)} %get-tuple-element.7) | copy-start | bytes 1572868
where the time goes:
time: 97.6 us; the launch traced here: 97 us
  Pallas kernels  92 us (94%)
  local copies, waits for them, and re-layouts  4.36 us (4%)
    pallas_call x1, Pallas kernels, front(): pl.pallas_call(functools.partial(front_kernel, spaces, cap), out_shape=[j...  32.8 us
    pallas_call x1, Pallas kernels, attention(): pl.pallas_call(attention_kernel, out_shape=[jax.ShapeDtypeStruct((rows, w...  31.5 us
    pallas_call x1, Pallas kernels, reduce_all(): pl.pallas_call(functools.partial(reduce_kernel, spaces, reps), out_shape=...  27.7 us

commit v1 on v0

--- a/solution.py
+++ b/solution.py
@@ -267,10 +267,94 @@
     )(features, neighbours, order, weight)
 
 
-def attention_kernel(reg, wi, wo, cot, att, grad, q, k, v, ctx):
+def attention_kernel(
+    spaces, reps, reg, wi, wo, cot, att, grad,
+    q, k, v, ctx, s0, s1, term, first, part, second, final, tail, tail_one, tail_two,
+    sa, ra, sb, rb, sc, rc, sd, rd, se, re,
+):
     rows, width = reg.shape
     head = width // HEADS
     half = width // 2
+    space, rep = lax.axis_index("space"), lax.axis_index("rep")
+    planes, others = spaces // 2, 2 * reps
+    chip, core = space // 2, space % 2
+    place = rep * 2 + core
+
+    def across(n):
+        return {"space": lax.rem(chip + n, planes) * 2 + core}
+
+    def along(n):
+        there = lax.rem(place + n, others)
+        return {"space": chip * 2 + there % 2, "rep": there // 2}
+
+    def run(count, make):
+        def body(n, carry):
+            make(n)
+            return carry
+
+        lax.fori_loop(1, count, body, 0)
+
+    barrier = pltpu.get_barrier_semaphore()
+    run(planes, lambda n: pl.semaphore_signal(barrier, inc=1, device_id=across(n), device_id_type=MESH))
+    run(others, lambda n: pl.semaphore_signal(barrier, inc=1, device_id=along(n), device_id_type=MESH))
+
+    def copy(src, dst, send, recv, device):
+        return pltpu.make_async_remote_copy(
+            src_ref=src, dst_ref=dst, send_sem=send, recv_sem=recv, device_id=device, device_id_type=MESH
+        )
+
+    def scatter(c, n):
+        return copy(term.at[c, lax.rem(chip + n, planes)], first.at[c, n], sa.at[c, n], ra.at[c, n], across(n))
+
+    def share(c, n):
+        return copy(part.at[c], second.at[c, place], sb.at[c, n], rb.at[c, n], along(n))
+
+    def shared(c, n):
+        there = lax.rem(place - n + others, others)
+        return copy(part.at[c], second.at[c, there], sb.at[c, n], rb.at[c, n], along(n))
+
+    def gather(c, n):
+        return copy(final.at[c, chip], final.at[c, chip], sc.at[c, n], rc.at[c, n], across(n))
+
+    def gathered(c, n):
+        there = lax.rem(chip - n + planes, planes)
+        return copy(final.at[c, there], final.at[c, there], sc.at[c, n], rc.at[c, n], across(n))
+
+    def share_tail(n):
+        return copy(tail.at[0], tail_one.at[place], sd.at[n], rd.at[n], along(n))
+
+    def shared_tail(n):
+        there = lax.rem(place - n + others, others)
+        return copy(tail.at[0], tail_one.at[there], sd.at[n], rd.at[n], along(n))
+
+    def gather_tail(n):
+        return copy(tail.at[1], tail_two.at[chip], se.at[n], re.at[n], across(n))
+
+    def gathered_tail(n):
+        there = lax.rem(chip - n + planes, planes)
+        return copy(tail.at[1], tail_two.at[there], se.at[n], re.at[n], across(n))
+
+    def finish_scatter(c):
+        first[c, 0] = term[c, chip]
+        run(planes, lambda n: scatter(c, n).wait())
+        part[c] = jnp.sum(first[c], axis=0)
+        run(others, lambda n: share(c, n).start())
+
+    def finish_share(c):
+        second[c, place] = part[c]
+        run(others, lambda n: share(c, n).wait_send())
+        run(others, lambda n: shared(c, n).wait_recv())
+        final[c, chip] = jnp.sum(second[c], axis=0)
+        run(planes, lambda n: gather(c, n).start())
+
+    def finish_gather(c):
+        run(planes, lambda n: gather(c, n).wait_send())
+        run(planes, lambda n: gathered(c, n).wait_recv())
+
+    def gradient_rows(side):
+        part_context = ctx[side].astype(BF16)
+        return lax.dot_general(part_context, cot[...], (((0,), (0,)), ((), ())), preferred_element_type=F32)
+
     residual = reg[...].astype(F32)
     centred = residual - jnp.mean(residual, axis=-1, keepdims=True)
     variance = jnp.mean(centred * centred, axis=-1, keepdims=True)
@@ -282,34 +366,89 @@
     for n in range(2):
         v[n] = jnp.concatenate([packed[:, 2 * width + n * half : 2 * width + (n + 1) * half], ones], axis=1)
     ctx[...] = jnp.zeros_like(ctx)
-    tile = 256
+    tile = s0.shape[0]
+    tiles = rows // tile
     lane_q = iota((tile, width), 1) // head
     lane_c = iota((tile, half), 1) // head
-
-    def one_head(h, carry):
+    held = (s0, s1)
+
+    def scores(h, t):
+        queries = jnp.where(lane_q == h, q[t * tile : (t + 1) * tile], jnp.zeros((), BF16))
+        return dot_t(queries, k[...])
+
+    def one_head(h):
         side = h // (HEADS // 2)
-        values = v[side]
-        for t in range(rows // tile):
+        for t in range(tiles):
+            later = h if t < tiles - 1 else jnp.minimum(h + 1, HEADS - 1)
+            held[(t + 1) % 2][...] = scores(later, (t + 1) % tiles)
+            now = held[t % 2][...]
+            lifted = jnp.exp(now - jnp.max(now, axis=-1, keepdims=True))
+            both = dot(lifted.astype(BF16), v[side])
             at = slice(t * tile, (t + 1) * tile)
-            queries = jnp.where(lane_q == h, q[at], jnp.zeros((), BF16))
-            scores = dot_t(queries, k[...])
-            lifted = jnp.exp(scores - jnp.max(scores, axis=-1, keepdims=True))
-            both = dot(lifted.astype(BF16), values)
-            ratio = both[:, :half] / both[:, half:]
-            ctx[side, at] += jnp.where(lane_c == h - side * (HEADS // 2), ratio, 0.0)
-        return carry
-
-    lax.fori_loop(0, HEADS, one_head, 0)
+            ctx[side, at] += jnp.where(lane_c == h - side * (HEADS // 2), both[:, :half] / both[:, half:], 0.0)
+
+    s0[...] = scores(0, 0)
+    blocks = term.shape[2]
+    steps = HEADS // 2
+
+    def step(n, carry):
+        one_head(2 * n)
+        one_head(2 * n + 1)
+
+        @pl.when(n == steps // 2 - 1)
+        def _():
+            term[0] = gradient_rows(0).reshape(planes, blocks, width)
+            pl.semaphore_wait(barrier, planes + others - 2)
+            run(planes, lambda m: scatter(0, m).start())
+
+        @pl.when(n == steps // 2)
+        def _():
+            finish_scatter(0)
+
+        @pl.when(n == steps // 2 + 1)
+        def _():
+            finish_share(0)
+
+        @pl.when(n == steps - 2)
+        def _():
+            term[1] = gradient_rows(1).reshape(planes, blocks, width)
+            run(planes, lambda m: scatter(1, m).start())
+
+        return carry
+
+    lax.fori_loop(0, steps, step, 0)
+    left = tail.shape[1]
+    tail[0] = gradient_rows(1)[half - left :]
+    run(others, lambda n: share_tail(n).start())
+    finish_scatter(1)
     context = jnp.concatenate([ctx[0], ctx[1]], axis=1).astype(BF16)
-    att[...] = (residual + dot(context, wo[...])).astype(BF16)
-    grad[...] = lax.dot_general(context, cot[...], (((0,), (0,)), ((), ())), preferred_element_type=F32)
+    att[...] = (reg[...].astype(F32) + dot(context, wo[...])).astype(BF16)
+    tail_one[place] = tail[0]
+    run(others, lambda n: share_tail(n).wait_send())
+    run(others, lambda n: shared_tail(n).wait_recv())
+    tail[1] = jnp.sum(tail_one[...], axis=0)
+    run(planes, lambda n: gather_tail(n).start())
+    finish_share(1)
+    finish_gather(0)
+    grad[:half] = final[0].reshape(half, width)
+    finish_gather(1)
+    grad[half : width - left] = final[1].reshape(half, width)[: half - left]
+    tail_two[chip] = tail[1]
+    run(planes, lambda n: gather_tail(n).wait_send())
+    run(planes, lambda n: gathered_tail(n).wait_recv())
+    grad[width - left :] = jnp.sum(tail_two[...], axis=0)
 
 
 def attention(regrouped, wi, wo, cot):
+    spaces, reps = lax.axis_size("space"), lax.axis_size("rep")
     rows, width = regrouped.shape
+    head, half = width // HEADS, width // 2
+    planes, others = spaces // 2, 2 * reps
+    block, left, tile = half // planes, 2 * head, 256
     vmem = pl.BlockSpec(memory_space=pltpu.VMEM)
+    dma = pltpu.SemaphoreType.DMA
     return pl.pallas_call(
-        attention_kernel,
+        functools.partial(attention_kernel, spaces, reps),
         out_shape=[jax.ShapeDtypeStruct((rows, width), BF16), jax.ShapeDtypeStruct((width, width), F32)],
         in_specs=[vmem] * 4,
         out_specs=[vmem, vmem],
@@ -317,9 +456,24 @@
             pltpu.VMEM((rows, width), BF16),
             pltpu.VMEM((rows, width), BF16),
             pltpu.VMEM((2, rows, width), BF16),
-            pltpu.VMEM((2, rows, width // 2), F32),
-        ],
-        compiler_params=pltpu.CompilerParams(vmem_limit_bytes=VMEM_LIMIT),
+            pltpu.VMEM((2, rows, half), F32),
+            pltpu.VMEM((tile, rows), F32),
+            pltpu.VMEM((tile, rows), F32),
+            pltpu.VMEM((2, planes, block, width), F32),
+            pltpu.VMEM((2, planes, block, width), F32),
+            pltpu.VMEM((2, block, width), F32),
+            pltpu.VMEM((2, others, block, width), F32),
+            pltpu.VMEM((2, planes, block, width), F32),
+            pltpu.VMEM((2, left, width), F32),
+            pltpu.VMEM((others, left, width), F32),
+            pltpu.VMEM((planes, left, width), F32),
+        ]
+        + [dma((2, planes))] * 2
+        + [dma((2, others))] * 2
+        + [dma((2, planes))] * 2
+        + [dma((others,))] * 2
+        + [dma((planes,))] * 2,
+        compiler_params=pltpu.CompilerParams(collective_id=1, has_side_effects=True, vmem_limit_bytes=VMEM_LIMIT),
         cost_estimate=pl.CostEstimate(
             flops=4 * HEADS * rows * rows * width, bytes_accessed=8 * rows * width, transcendentals=HEADS * rows * rows
         ),
@@ -327,117 +481,9 @@
     )(regrouped, wi, wo, cot)
 
 
-def reduce_kernel(spaces, reps, term, out, first, second, part, sum_all, s1, r1, s2, r2, s3, r3, s4, r4):
-    space, rep = lax.axis_index("space"), lax.axis_index("rep")
-    planes = spaces // 2
-    chip, core = space // 2, space % 2
-    others = 2 * reps
-    place = rep * 2 + core
-
-    def across(n):
-        return {"space": lax.rem(chip + n, planes) * 2 + core}
-
-    def along(n):
-        there = lax.rem(place + n, others)
-        return {"space": chip * 2 + there % 2, "rep": there // 2}
-
-    barrier = pltpu.get_barrier_semaphore()
-
-    def greet_a(n, carry):
-        pl.semaphore_signal(barrier, inc=1, device_id=across(n), device_id_type=MESH)
-        return carry
-
-    def greet_b(n, carry):
-        pl.semaphore_signal(barrier, inc=1, device_id=along(n), device_id_type=MESH)
-        return carry
-
-    lax.fori_loop(1, planes, greet_a, 0)
-    lax.fori_loop(1, others, greet_b, 0)
-    pl.semaphore_wait(barrier, planes + others - 2)
-
-    def copy(src, dst, sems, n, device):
-        return pltpu.make_async_remote_copy(
-            src_ref=src, dst_ref=dst, send_sem=sems[0].at[n], recv_sem=sems[1].at[n], device_id=device, device_id_type=MESH
-        )
-
-    def c1(n):
-        there = lax.rem(chip + n, planes)
-        return copy(term.at[there], first.at[n], (s1, r1), n, across(n))
-
-    def c2(n):
-        there = lax.rem(place + n, others)
-        return copy(part.at[there], second.at[n], (s2, r2), n, along(n))
-
-    def c3(n):
-        return copy(sum_all.at[chip, place], sum_all.at[chip, place], (s3, r3), n, along(n))
-
-    def w3(n):
-        there = lax.rem(place - n + others, others)
-        return copy(sum_all.at[chip, there], sum_all.at[chip, there], (s3, r3), n, along(n))
-
-    def c4(n):
-        return copy(sum_all.at[chip], sum_all.at[chip], (s4, r4), n, across(n))
-
-    def w4(n):
-        there = lax.rem(chip - n + planes, planes)
-        return copy(sum_all.at[there], sum_all.at[there], (s4, r4), n, across(n))
-
-    def run(count, make):
-        def body(n, carry):
-            make(n)
-            return carry
-
-        lax.fori_loop(1, count, body, 0)
-
-    run(planes, lambda n: c1(n).start())
-    first[0] = term[chip]
-    run(planes, lambda n: c1(n).wait())
-    part[...] = jnp.sum(first[...], axis=0)
-    run(others, lambda n: c2(n).start())
-    second[0] = part[place]
-    run(others, lambda n: c2(n).wait())
-    sum_all[chip, place] = jnp.sum(second[...], axis=0)
-    run(others, lambda n: c3(n).start())
-    run(others, lambda n: c3(n).wait_send())
-    run(others, lambda n: w3(n).wait_recv())
-    run(planes, lambda n: c4(n).start())
-    run(planes, lambda n: c4(n).wait_send())
-    run(planes, lambda n: w4(n).wait_recv())
-    out[...] = sum_all[...]
-
-
-def reduce_all(term):
-    spaces, reps = lax.axis_size("space"), lax.axis_size("rep")
-    rows, width = term.shape
-    planes, others = spaces // 2, 2 * reps
-    small = rows // planes // others
-    sub = small * width // 128
-    shape = (planes, others, sub, 128)
-    vmem = pl.BlockSpec(memory_space=pltpu.VMEM)
-    out = pl.pallas_call(
-        functools.partial(reduce_kernel, spaces, reps),
-        out_shape=jax.ShapeDtypeStruct(shape, F32),
-        in_specs=[vmem],
-        out_specs=vmem,
-        scratch_shapes=[
-            pltpu.VMEM((planes, others, sub, 128), F32),
-            pltpu.VMEM((others, sub, 128), F32),
-            pltpu.VMEM((others, sub, 128), F32),
-            pltpu.VMEM(shape, F32),
-        ]
-        + [pltpu.SemaphoreType.DMA((planes,))] * 2
-        + [pltpu.SemaphoreType.DMA((others,))] * 4
-        + [pltpu.SemaphoreType.DMA((planes,))] * 2,
-        compiler_params=pltpu.CompilerParams(collective_id=1, has_side_effects=True),
-        name="reduce_all",
-    )(term.reshape(shape))
-    return out.reshape(rows, width)
-
-
 def local(features, neighbours, serial_order, kernel_weight, input_projection, output_projection, cotangent):
     encoded, regrouped = front(features[0], neighbours[0], serial_order, kernel_weight)
-    attended, term = attention(regrouped, input_projection, output_projection, cotangent[0])
-    gradient = reduce_all(term)
+    attended, gradient = attention(regrouped, input_projection, output_projection, cotangent[0])
     return encoded[None], attended[None], gradient
 
 

time: 97.6 us -> 88.6 us (0.908)
  Pallas kernels: 92 us -> 83.3 us
    pallas_call x2 -> x1, Pallas kernels: 59.2 us -> 50.5 us  [attention(): pl.pallas_call(functools.partial(attention_kernel, spaces, reps), out_sha...]
    reshape x2 -> x0, local copies, waits for them, and re-layouts: 3.56 us -> none  [the longest x1 1.79 us: reduce_all(): return out.reshape(rows, width)]
    unnamed x3 -> x5, local copies, waits for them, and re-layouts: 0.8 us -> 4.34 us
where the time goes in v1:
time: 88.6 us; the launch traced here: 88.3 us
  Pallas kernels  83.3 us (94%)
  local copies, waits for them, and re-layouts  4.34 us (5%)
    pallas_call x1, Pallas kernels, attention(): pl.pallas_call(functools.partial(attention_kernel, spaces, reps), out_sha...  50.5 us
    pallas_call x1, Pallas kernels, front(): pl.pallas_call(functools.partial(front_kernel, spaces, cap), out_shape=[j...  32.8 us
    unnamed x5, local copies, waits for them, and re-layouts  4.34 us

profile of v1, /device:TPU:1, one launch (start us, length us, event | category | flops | bytes accessed | tf_op | source)
XLA Modules:
  0.0 88.3 jit_solution(10884954650179801699)
XLA Ops:
  0.6 32.8 %front.1 = (bf16[1024,256]{1,0:T(8,128)(2,1)}, bf16[1024,256]{1,0:T(8,128)(2,1)}) custom-call(bf16[1024,256]{1,0:T(8,128)(2,1)} %bitcast.7, s32[2,26]{1,0:T(2,128)} %bitcast.9, s32[1,1024]{1,0:T(1,128)} %order.1, bf16[27,256,256]{2,1,0:T(8,128)(2,1)} %w_hbm.1), custom_call_target="tpu_custom_call" | custom-call | flops 3623878656 | bytes 5111808 | tf_op jit(solution)/shard_map/front/pallas_call | solution.py:240
  33.5 0.0 copy-start
  33.5 50.5 %attention.1 = (bf16[1024,256]{1,0:T(8,128)(2,1)}, f32[256,256]{1,0:T(8,128)}) custom-call(bf16[1024,256]{1,0:T(8,128)(2,1)} %get-tuple-element.8.reg, bf16[256,768]{1,0:T(8,128)(2,1)} %wi.1, bf16[256,256]{1,0:T(8,128)(2,1)} %wo.1, bf16[1024,256]{1,0:T(8,128)(2,1)} %bitcast.8), custom_call_target="tpu_custom_call" | custom-call | flops 17179869184 | bytes 2097152 | tf_op jit(solution)/shard_map/attention/pallas_call | solution.py:450
  84.0 0.0 copy-done
  84.0 0.8 copy.13
  84.8 1.9 %copy.14 = bf16[1,1024,256]{2,1,0:T(8,128)(2,1)} copy(bf16[1,1024,256]{2,1,0:T(8,128)(2,1)} %bitcast.6) | data formatting | bytes 1048576
  86.7 1.7 %copy.15 = f32[256,256]{1,0:T(8,128)} copy(f32[256,256]{1,0:T(8,128)} %get-tuple-element.16) | data formatting | bytes 524288
Async XLA Ops:
  33.5 50.5 %copy-start = (bf16[1024,256]{1,0:T(8,128)(2,1)S(1)}, bf16[1024,256]{1,0:T(8,128)(2,1)}, u32[]{:S(2)}) copy-start(bf16[1024,256]{1,0:T(8,128)(2,1)} %get-tuple-element.7) | copy-start | bytes 1572868

commit v2 on v1

--- a/solution.py
+++ b/solution.py
@@ -33,7 +33,7 @@
 
 def front_kernel(
     spaces, cap, feat, nb, order, w_hbm, enc, reg,
-    w, x, halo_l, halo_r, table, got, send, recv,
+    w, x, halo_l, halo_r, table, got, send, recv, place,
     w_sem, hs, hr, ts, tr, rs, rr,
 ):
     me = lax.axis_index("space")
@@ -54,58 +54,6 @@
         return carry
 
     lax.fori_loop(1, spaces, greet, 0)
-
-    places = order[...]
-    shift = rows.bit_length() - 1
-    owner = lax.shift_right_logical(places, shift)
-    slot = places & (rows - 1)
-    ahead = (owner - me + spaces) & (spaces - 1)
-    chosen = jnp.where(iota((spaces, rows), 0) == ahead, 1.0, 0.0)
-    before = onehot(iota((rows, rows), 0) < iota((rows, rows), 1))
-    rank = jnp.sum(chosen * dot(chosen.astype(BF16), before), axis=0, keepdims=True)
-    high = lax.shift_right_logical(slot, 5).astype(F32)
-    low = (slot & 31).astype(F32)
-    lanes = table.shape[2]
-    by_rank = onehot(iota((lanes, rows), 0).astype(F32) == rank)
-    stacked = jnp.concatenate([chosen * high, chosen * low, chosen], axis=0).astype(BF16)
-    found = dot_t(stacked, by_rank)
-    slots = found[:spaces] * 32.0 + found[spaces : 2 * spaces]
-    slots = jnp.where(found[2 * spaces :] > 0.5, slots, -1.0)
-    table[...] = jnp.broadcast_to(slots[:, None, :], table.shape)
-    row_at = ahead.astype(F32) * float(cap) + rank
-
-    pl.semaphore_wait(barrier, spaces - 1)
-
-    halos = []
-    for b in range(bricks):
-        for source, dst, step, n in (
-            (b * brick + brick - face, halo_l, 1, 2 * b),
-            (b * brick, halo_r, spaces - 1, 2 * b + 1),
-        ):
-            copy = pltpu.make_async_remote_copy(
-                src_ref=feat.at[pl.ds(source, face)], dst_ref=dst.at[b], send_sem=hs.at[n], recv_sem=hr.at[n],
-                device_id=peer(step), device_id_type=MESH,
-            )
-            copy.start()
-            halos.append(copy)
-
-    def table_copy(k):
-        return pltpu.make_async_remote_copy(
-            src_ref=table.at[k], dst_ref=got.at[k], send_sem=ts.at[k], recv_sem=tr.at[k],
-            device_id=peer(k), device_id_type=MESH,
-        )
-
-    def row_copy(k):
-        return pltpu.make_async_remote_copy(
-            src_ref=send.at[k], dst_ref=recv.at[k], send_sem=rs.at[k], recv_sem=rr.at[k],
-            device_id=peer(k), device_id_type=MESH,
-        )
-
-    def start_table(k, carry):
-        table_copy(k).start()
-        return carry
-
-    lax.fori_loop(1, spaces, start_table, 0)
 
     depth = iota((EDGE + 2, EDGE, width), 1)
 
@@ -160,6 +108,76 @@
 
     lax.fori_loop(0, EDGE, inner, 0)
 
+    places = order[...]
+    shift = rows.bit_length() - 1
+    owner = lax.shift_right_logical(places, shift)
+    slot = places & (rows - 1)
+    ahead = (owner - me + spaces) & (spaces - 1)
+    chosen = jnp.where(iota((spaces, rows), 0) == ahead, 1.0, 0.0)
+    before = onehot(iota((rows, rows), 0) < iota((rows, rows), 1))
+    rank = jnp.sum(chosen * dot(chosen.astype(BF16), before), axis=0, keepdims=True)
+    high = lax.shift_right_logical(slot, 5).astype(F32)
+    low = (slot & 31).astype(F32)
+    lanes = table.shape[2]
+    by_rank = onehot(iota((lanes, rows), 0).astype(F32) == rank)
+    stacked = jnp.concatenate([chosen * high, chosen * low, chosen], axis=0).astype(BF16)
+    found = dot_t(stacked, by_rank)
+    slots = found[:spaces] * 32.0 + found[spaces : 2 * spaces]
+    slots = jnp.where(found[2 * spaces :] > 0.5, slots, -1.0)
+    table[...] = jnp.broadcast_to(slots[:, None, :], table.shape)
+    row_at = ahead.astype(F32) * float(cap) + rank
+
+    pl.semaphore_wait(barrier, spaces - 1)
+
+    halos = []
+    for b in range(bricks):
+        for source, dst, step, n in (
+            (b * brick + brick - face, halo_l, 1, 2 * b),
+            (b * brick, halo_r, spaces - 1, 2 * b + 1),
+        ):
+            copy = pltpu.make_async_remote_copy(
+                src_ref=feat.at[pl.ds(source, face)], dst_ref=dst.at[b], send_sem=hs.at[n], recv_sem=hr.at[n],
+                device_id=peer(step), device_id_type=MESH,
+            )
+            copy.start()
+            halos.append(copy)
+
+    def table_copy(k):
+        return pltpu.make_async_remote_copy(
+            src_ref=table.at[k], dst_ref=got.at[k], send_sem=ts.at[k], recv_sem=tr.at[k],
+            device_id=peer(k), device_id_type=MESH,
+        )
+
+    def row_copy(k):
+        return pltpu.make_async_remote_copy(
+            src_ref=send.at[k], dst_ref=recv.at[k], send_sem=rs.at[k], recv_sem=rr.at[k],
+            device_id=peer(k), device_id_type=MESH,
+        )
+
+    def start_table(k, carry):
+        table_copy(k).start()
+        return carry
+
+    lax.fori_loop(1, spaces, start_table, 0)
+
+    def window(first, count, p):
+        return pl.ds(first + p * face if isinstance(first, int) else pl.multiple_of(first + p * face, face), count)
+
+    def products(p, rows_in):
+        return dot(rows_in, w[9 * p : 9 * p + 9].reshape(9 * width, width))
+
+    load.wait()
+    middle = brick - 2 * face
+
+    def conv_middle(b, carry):
+        acc = jnp.zeros((middle, width), F32)
+        for p in range(3):
+            acc = acc + products(p, x[b, window(face, middle, p), :])
+        at = pl.ds(pl.multiple_of(b * brick + face, face), middle)
+        enc[at] = (feat[at].astype(F32) + acc).astype(BF16)
+        return carry
+
+    lax.fori_loop(0, bricks, conv_middle, 0)
     for copy in halos:
         copy.wait_recv()
     tops = [layer(feat, n * brick + brick - face) for n in range(bricks)]
@@ -170,20 +188,13 @@
         write_layer(b, 0, -1, lefts + tops, left_ids + own_ids, None)
         write_layer(b, EDGE + 1, 1, bottoms + rights, own_ids + right_ids, None)
 
-    load.wait()
-    tile = 256
-
-    def conv(n, carry):
-        b, first = n // (brick // tile), n % (brick // tile) * tile
-        acc = jnp.zeros((tile, width), F32)
-        for p in range(3):
-            window = x[b, pl.ds(pl.multiple_of(first + p * face, face), tile), :]
-            acc = acc + dot(window, w[9 * p : 9 * p + 9].reshape(9 * width, width))
-        at = pl.ds(pl.multiple_of(n * tile, tile), tile)
-        enc[at] = (feat[at].astype(F32) + acc).astype(BF16)
-        return carry
-
-    lax.fori_loop(0, rows // tile, conv, 0)
+    ends = [(b, first) for b in range(bricks) for first in (0, brick - face)]
+    acc = jnp.zeros((len(ends) * face, width), F32)
+    for p in range(3):
+        acc = acc + products(p, jnp.concatenate([x[b, window(first, face, p), :] for b, first in ends], axis=0))
+    for n, (b, first) in enumerate(ends):
+        at = pl.ds(b * brick + first, face)
+        enc[at] = (feat[at].astype(F32) + acc[n * face : (n + 1) * face]).astype(BF16)
 
     group = 8
     for c in range(spaces // group):
@@ -200,25 +211,24 @@
         return carry
 
     lax.fori_loop(1, spaces, wait_table, 0)
+    column = iota((8, 128), 1)
+    for t in range(spaces * cap // 128):
+        lane = jnp.full((8, 128), -1.0, F32)
+        for k in range(spaces):
+            start, end = max(0, k * cap - 128 * t), min(128, (k + 1) * cap - 128 * t)
+            if start >= end:
+                continue
+            moved = got[k]
+            if (k * cap - 128 * t) % 128:
+                moved = pltpu.roll(moved, (k * cap - 128 * t) % 128, 1)
+            lane = jnp.where((column >= start) & (column < end), moved, lane)
+        place[:, t * 128 : (t + 1) * 128] = onehot(iota((rows, 128), 0).astype(F32) == lane[0:1])
     total = jnp.zeros((rows, width), F32)
-    column = iota((8, 128), 1)
     for c in range(spaces // group):
         for k in range(max(1, c * group), (c + 1) * group):
             row_copy(k).wait_recv()
-        blocks = []
-        for t in range(c * group * cap // 128, (c + 1) * group * cap // 128):
-            lane = jnp.full((8, 128), -1.0, F32)
-            for k in range(spaces):
-                start, end = max(0, k * cap - 128 * t), min(128, (k + 1) * cap - 128 * t)
-                if start >= end:
-                    continue
-                moved = got[k]
-                if (k * cap - 128 * t) % 128:
-                    moved = pltpu.roll(moved, (k * cap - 128 * t) % 128, 1)
-                lane = jnp.where((column >= start) & (column < end), moved, lane)
-            blocks.append(onehot(iota((rows, 128), 0).astype(F32) == lane[0:1]))
         arrived = recv[c * group : (c + 1) * group].reshape(group * cap, width)
-        total = total + dot(jnp.concatenate(blocks, axis=1), arrived)
+        total = total + dot(place[:, c * group * cap : (c + 1) * group * cap], arrived)
     reg[...] = total.astype(BF16)
 
     def wait_sent(k, carry):
@@ -251,6 +261,7 @@
             pltpu.VMEM((spaces, 8, 128), F32),
             pltpu.VMEM((spaces, cap, width), BF16),
             pltpu.VMEM((spaces, cap, width), BF16),
+            pltpu.VMEM((rows, spaces * cap), BF16),
             pltpu.SemaphoreType.DMA,
             pltpu.SemaphoreType.DMA((2 * bricks,)),
             pltpu.SemaphoreType.DMA((2 * bricks,)),
@@ -401,13 +412,9 @@
             pl.semaphore_wait(barrier, planes + others - 2)
             run(planes, lambda m: scatter(0, m).start())
 
-        @pl.when(n == steps // 2)
+        @pl.when(n == steps // 2 + 1)
         def _():
             finish_scatter(0)
-
-        @pl.when(n == steps // 2 + 1)
-        def _():
-            finish_share(0)
 
         @pl.when(n == steps - 2)
         def _():
@@ -418,15 +425,16 @@
 
     lax.fori_loop(0, steps, step, 0)
     left = tail.shape[1]
-    tail[0] = gradient_rows(1)[half - left :]
+    tail[0] = gradient_rows(1)[half - left :].astype(BF16)
     run(others, lambda n: share_tail(n).start())
-    finish_scatter(1)
+    finish_share(0)
     context = jnp.concatenate([ctx[0], ctx[1]], axis=1).astype(BF16)
     att[...] = (reg[...].astype(F32) + dot(context, wo[...])).astype(BF16)
+    finish_scatter(1)
     tail_one[place] = tail[0]
     run(others, lambda n: share_tail(n).wait_send())
     run(others, lambda n: shared_tail(n).wait_recv())
-    tail[1] = jnp.sum(tail_one[...], axis=0)
+    tail[1] = jnp.sum(tail_one[...].astype(F32), axis=0).astype(BF16)
     run(planes, lambda n: gather_tail(n).start())
     finish_share(1)
     finish_gather(0)
@@ -436,7 +444,7 @@
     tail_two[chip] = tail[1]
     run(planes, lambda n: gather_tail(n).wait_send())
     run(planes, lambda n: gathered_tail(n).wait_recv())
-    grad[width - left :] = jnp.sum(tail_two[...], axis=0)
+    grad[width - left :] = jnp.sum(tail_two[...].astype(F32), axis=0)
 
 
 def attention(regrouped, wi, wo, cot):
@@ -464,9 +472,9 @@
             pltpu.VMEM((2, block, width), F32),
             pltpu.VMEM((2, others, block, width), F32),
             pltpu.VMEM((2, planes, block, width), F32),
-            pltpu.VMEM((2, left, width), F32),
-            pltpu.VMEM((others, left, width), F32),
-            pltpu.VMEM((planes, left, width), F32),
+            pltpu.VMEM((2, left, width), BF16),
+            pltpu.VMEM((others, left, width), BF16),
+            pltpu.VMEM((planes, left, width), BF16),
         ]
         + [dma((2, planes))] * 2
         + [dma((2, others))] * 2
@@ -481,9 +489,30 @@
     )(regrouped, wi, wo, cot)
 
 
+def publish_kernel(count, *refs):
+    copies = [pltpu.make_async_copy(refs[n], refs[count + n], refs[2 * count].at[n]) for n in range(count)]
+    for copy in copies:
+        copy.start()
+    for copy in copies:
+        copy.wait()
+
+
+def publish(*arrays):
+    spec = pl.BlockSpec(memory_space=pl.ANY)
+    return pl.pallas_call(
+        functools.partial(publish_kernel, len(arrays)),
+        out_shape=[jax.ShapeDtypeStruct(a.shape, a.dtype) for a in arrays],
+        in_specs=[spec] * len(arrays),
+        out_specs=[spec] * len(arrays),
+        scratch_shapes=[pltpu.SemaphoreType.DMA((len(arrays),))],
+        name="publish",
+    )(*arrays)
+
+
 def local(features, neighbours, serial_order, kernel_weight, input_projection, output_projection, cotangent):
     encoded, regrouped = front(features[0], neighbours[0], serial_order, kernel_weight)
     attended, gradient = attention(regrouped, input_projection, output_projection, cotangent[0])
+    encoded, attended, gradient = publish(encoded, attended, gradient)
     return encoded[None], attended[None], gradient
 
 

time: 88.6 us -> 116 us (1.31)
  Pallas kernels: 83.3 us -> 115 us
  local copies, waits for them, and re-layouts: 4.34 us -> 0 us
    pallas_call x0 -> x1, Pallas kernels: none -> 40.8 us  [publish(): pl.pallas_call(functools.partial(publish_kernel, len(arrays)), out_shape=...]
    pallas_call x1, Pallas kernels: 50.5 us -> 44 us  [attention(): pl.pallas_call(functools.partial(attention_kernel, spaces, reps), out_sha...]
    unnamed x5 -> x0, local copies, waits for them, and re-layouts: 4.34 us -> none
    pallas_call x1, Pallas kernels: 32.8 us -> 30.1 us  [front(): pl.pallas_call(functools.partial(front_kernel, spaces, cap), out_shape=[j...]
where the time goes in v2:
time: 116 us
  Pallas kernels  115 us (99%)
    pallas_call x1, Pallas kernels, attention(): pl.pallas_call(functools.partial(attention_kernel, spaces, reps), out_sha...  44 us
    pallas_call x1, Pallas kernels, publish(): pl.pallas_call(functools.partial(publish_kernel, len(arrays)), out_shape=...  40.8 us
    pallas_call x1, Pallas kernels, front(): pl.pallas_call(functools.partial(front_kernel, spaces, cap), out_shape=[j...  30.1 us

profile of v2, /device:TPU:1, one launch (start us, length us, event | category | flops | bytes accessed | tf_op | source)
XLA Modules:
  0.0 115.5 jit_solution(676376559066119844)
XLA Ops:
  0.6 30.1 %front.1 = (bf16[1024,256]{1,0:T(8,128)(2,1)}, bf16[1024,256]{1,0:T(8,128)(2,1)}) custom-call(bf16[1024,256]{1,0:T(8,128)(2,1)} %bitcast.5, s32[2,26]{1,0:T(2,128)} %bitcast.9, s32[1,1024]{1,0:T(1,128)} %order.1, bf16[27,256,256]{2,1,0:T(8,128)(2,1)} %w_hbm.1), custom_call_target="tpu_custom_call" | custom-call | flops 3623878656 | bytes 5111808 | tf_op jit(solution)/shard_map/front/pallas_call | solution.py:250
  30.7 44.0 %attention.1 = (bf16[1024,256]{1,0:T(8,128)(2,1)}, f32[256,256]{1,0:T(8,128)}) custom-call(bf16[1024,256]{1,0:T(8,128)(2,1)} %get-tuple-element.11.reg, bf16[256,768]{1,0:T(8,128)(2,1)} %wi.1, bf16[256,256]{1,0:T(8,128)(2,1)} %wo.1, bf16[1024,256]{1,0:T(8,128)(2,1)} %bitcast.6), custom_call_target="tpu_custom_call" | custom-call | flops 17179869184 | bytes 2097152 | tf_op jit(solution)/shard_map/attention/pallas_call | solution.py:458
  74.7 40.8 %publish.1 = (bf16[1024,256]{1,0:T(8,128)(2,1)}, bf16[1024,256]{1,0:T(8,128)(2,1)}, f32[256,256]{1,0:T(8,128)}) custom-call(bf16[1024,256]{1,0:T(8,128)(2,1)} %get-tuple-element.10.refs_0_, bf16[1024,256]{1,0:T(8,128)(2,1)} %get-tuple-element.12.refs_1_, f32[256,256]{1,0:T(8,128)} %get-tuple-element.13.refs_2_), custom_call_target="tpu_custom_call" | custom-call | tf_op jit(solution)/shard_map/publish/pallas_call | solution.py:502

commit v3 on v2

--- a/solution.py
+++ b/solution.py
@@ -280,9 +280,9 @@
 
 def attention_kernel(
     spaces, reps, reg, wi, wo, cot, att, grad,
-    q, k, v, ctx, s0, s1, term, first, part, second, final, tail, tail_one, tail_two,
-    sa, ra, sb, rb, sc, rc, sd, rd, se, re,
+    q, k, v, ctx, s0, s1, *comm,
 ):
+    chunks = [comm[n : n + 11] for n in range(0, len(comm), 11)]
     rows, width = reg.shape
     head = width // HEADS
     half = width // 2
@@ -315,52 +315,41 @@
         )
 
     def scatter(c, n):
-        return copy(term.at[c, lax.rem(chip + n, planes)], first.at[c, n], sa.at[c, n], ra.at[c, n], across(n))
-
-    def share(c, n):
-        return copy(part.at[c], second.at[c, place], sb.at[c, n], rb.at[c, n], along(n))
-
-    def shared(c, n):
-        there = lax.rem(place - n + others, others)
-        return copy(part.at[c], second.at[c, there], sb.at[c, n], rb.at[c, n], along(n))
-
-    def gather(c, n):
-        return copy(final.at[c, chip], final.at[c, chip], sc.at[c, n], rc.at[c, n], across(n))
-
-    def gathered(c, n):
-        there = lax.rem(chip - n + planes, planes)
-        return copy(final.at[c, there], final.at[c, there], sc.at[c, n], rc.at[c, n], across(n))
-
-    def share_tail(n):
-        return copy(tail.at[0], tail_one.at[place], sd.at[n], rd.at[n], along(n))
-
-    def shared_tail(n):
-        there = lax.rem(place - n + others, others)
-        return copy(tail.at[0], tail_one.at[there], sd.at[n], rd.at[n], along(n))
-
-    def gather_tail(n):
-        return copy(tail.at[1], tail_two.at[chip], se.at[n], re.at[n], across(n))
-
-    def gathered_tail(n):
-        there = lax.rem(chip - n + planes, planes)
-        return copy(tail.at[1], tail_two.at[there], se.at[n], re.at[n], across(n))
-
-    def finish_scatter(c):
-        first[c, 0] = term[c, chip]
-        run(planes, lambda n: scatter(c, n).wait())
-        part[c] = jnp.sum(first[c], axis=0)
-        run(others, lambda n: share(c, n).start())
-
-    def finish_share(c):
-        second[c, place] = part[c]
-        run(others, lambda n: share(c, n).wait_send())
-        run(others, lambda n: shared(c, n).wait_recv())
-        final[c, chip] = jnp.sum(second[c], axis=0)
-        run(planes, lambda n: gather(c, n).start())
-
-    def finish_gather(c):
-        run(planes, lambda n: gather(c, n).wait_send())
-        run(planes, lambda n: gathered(c, n).wait_recv())
+        term, first, part, second, final, s1, r1, s2, r2, s3, r3 = chunks[c]
+        return copy(term.at[lax.rem(place + n, others)], first.at[n], s1.at[n], r1.at[n], along(n))
+
+    def share(c, n, sender):
+        term, first, part, second, final, s1, r1, s2, r2, s3, r3 = chunks[c]
+        return copy(part, second.at[sender], s2.at[n], r2.at[n], across(n))
+
+    def gather(c, n, sender):
+        term, first, part, second, final, s1, r1, s2, r2, s3, r3 = chunks[c]
+        return copy(final.at[sender], final.at[sender], s3.at[n], r3.at[n], along(n))
+
+    def start_scatter(c, values):
+        chunks[c][0][...] = values.reshape(chunks[c][0].shape)
+        run(others, lambda n: scatter(c, n).start())
+
+    def start_share(c):
+        term, first, part, second = chunks[c][:4]
+        first[0] = term[place]
+        run(others, lambda n: scatter(c, n).wait())
+        part[...] = jnp.sum(first[...], axis=0)
+        run(planes, lambda n: share(c, n, chip).start())
+
+    def start_gather(c):
+        part, second, final = chunks[c][2:5]
+        second[chip] = part[...]
+        run(planes, lambda n: share(c, n, chip).wait_send())
+        run(planes, lambda n: share(c, n, lax.rem(chip - n + planes, planes)).wait_recv())
+        final[place] = jnp.sum(second[...], axis=0)
+        run(others, lambda n: gather(c, n, place).start())
+
+    def finish(c, at):
+        final = chunks[c][4]
+        run(others, lambda n: gather(c, n, place).wait_send())
+        run(others, lambda n: gather(c, n, lax.rem(place - n + others, others)).wait_recv())
+        grad[at] = final[...].reshape(-1, width)
 
     def gradient_rows(side):
         part_context = ctx[side].astype(BF16)
@@ -399,60 +388,45 @@
             ctx[side, at] += jnp.where(lane_c == h - side * (HEADS // 2), both[:, :half] / both[:, half:], 0.0)
 
     s0[...] = scores(0, 0)
-    blocks = term.shape[2]
-    steps = HEADS // 2
+    heads_a_step = HEADS // 4
 
     def step(n, carry):
-        one_head(2 * n)
-        one_head(2 * n + 1)
-
-        @pl.when(n == steps // 2 - 1)
+        for m in range(heads_a_step):
+            one_head(heads_a_step * n + m)
+
+        @pl.when(n == 1)
         def _():
-            term[0] = gradient_rows(0).reshape(planes, blocks, width)
+            values = gradient_rows(0)
             pl.semaphore_wait(barrier, planes + others - 2)
-            run(planes, lambda m: scatter(0, m).start())
-
-        @pl.when(n == steps // 2 + 1)
+            start_scatter(0, values)
+
+        @pl.when(n == 2)
         def _():
-            finish_scatter(0)
-
-        @pl.when(n == steps - 2)
-        def _():
-            term[1] = gradient_rows(1).reshape(planes, blocks, width)
-            run(planes, lambda m: scatter(1, m).start())
-
-        return carry
-
-    lax.fori_loop(0, steps, step, 0)
-    left = tail.shape[1]
-    tail[0] = gradient_rows(1)[half - left :].astype(BF16)
-    run(others, lambda n: share_tail(n).start())
-    finish_share(0)
+            start_scatter(1, gradient_rows(1)[: half // 2])
+            start_share(0)
+
+        return carry
+
+    lax.fori_loop(0, 4, step, 0)
+    start_scatter(2, gradient_rows(1)[half // 2 :])
+    start_share(1)
+    start_gather(0)
     context = jnp.concatenate([ctx[0], ctx[1]], axis=1).astype(BF16)
     att[...] = (reg[...].astype(F32) + dot(context, wo[...])).astype(BF16)
-    finish_scatter(1)
-    tail_one[place] = tail[0]
-    run(others, lambda n: share_tail(n).wait_send())
-    run(others, lambda n: shared_tail(n).wait_recv())
-    tail[1] = jnp.sum(tail_one[...].astype(F32), axis=0).astype(BF16)
-    run(planes, lambda n: gather_tail(n).start())
-    finish_share(1)
-    finish_gather(0)
-    grad[:half] = final[0].reshape(half, width)
-    finish_gather(1)
-    grad[half : width - left] = final[1].reshape(half, width)[: half - left]
-    tail_two[chip] = tail[1]
-    run(planes, lambda n: gather_tail(n).wait_send())
-    run(planes, lambda n: gathered_tail(n).wait_recv())
-    grad[width - left :] = jnp.sum(tail_two[...].astype(F32), axis=0)
+    start_share(2)
+    start_gather(1)
+    finish(0, slice(0, half))
+    start_gather(2)
+    finish(1, slice(half, half + half // 2))
+    finish(2, slice(half + half // 2, width))
 
 
 def attention(regrouped, wi, wo, cot):
     spaces, reps = lax.axis_size("space"), lax.axis_size("rep")
     rows, width = regrouped.shape
-    head, half = width // HEADS, width // 2
+    half = width // 2
     planes, others = spaces // 2, 2 * reps
-    block, left, tile = half // planes, 2 * head, 256
+    tile = 256
     vmem = pl.BlockSpec(memory_space=pltpu.VMEM)
     dma = pltpu.SemaphoreType.DMA
     return pl.pallas_call(
@@ -467,20 +441,21 @@
             pltpu.VMEM((2, rows, half), F32),
             pltpu.VMEM((tile, rows), F32),
             pltpu.VMEM((tile, rows), F32),
-            pltpu.VMEM((2, planes, block, width), F32),
-            pltpu.VMEM((2, planes, block, width), F32),
-            pltpu.VMEM((2, block, width), F32),
-            pltpu.VMEM((2, others, block, width), F32),
-            pltpu.VMEM((2, planes, block, width), F32),
-            pltpu.VMEM((2, left, width), BF16),
-            pltpu.VMEM((others, left, width), BF16),
-            pltpu.VMEM((planes, left, width), BF16),
         ]
-        + [dma((2, planes))] * 2
-        + [dma((2, others))] * 2
-        + [dma((2, planes))] * 2
-        + [dma((others,))] * 2
-        + [dma((planes,))] * 2,
+        + [
+            spec
+            for count in (half, half // 2, half // 2)
+            for spec in (
+                pltpu.VMEM((others, count // others, width), F32),
+                pltpu.VMEM((others, count // others, width), F32),
+                pltpu.VMEM((count // others, width), F32),
+                pltpu.VMEM((planes, count // others, width), F32),
+                pltpu.VMEM((others, count // others, width), F32),
+                *[dma((others,))] * 2,
+                *[dma((planes,))] * 2,
+                *[dma((others,))] * 2,
+            )
+        ],
         compiler_params=pltpu.CompilerParams(collective_id=1, has_side_effects=True, vmem_limit_bytes=VMEM_LIMIT),
         cost_estimate=pl.CostEstimate(
             flops=4 * HEADS * rows * rows * width, bytes_accessed=8 * rows * width, transcendentals=HEADS * rows * rows
@@ -490,11 +465,16 @@
 
 
 def publish_kernel(count, *refs):
-    copies = [pltpu.make_async_copy(refs[n], refs[count + n], refs[2 * count].at[n]) for n in range(count)]
-    for copy in copies:
-        copy.start()
-    for copy in copies:
-        copy.wait()
+    given, made, held, sems = refs[:count], refs[count : 2 * count], refs[2 * count : 3 * count], refs[3 * count]
+    reads = [pltpu.make_async_copy(given[n], held[n], sems.at[0, n]) for n in range(count)]
+    writes = [pltpu.make_async_copy(held[n], made[n], sems.at[1, n]) for n in range(count)]
+    for read in reads:
+        read.start()
+    for read, write in zip(reads, writes):
+        read.wait()
+        write.start()
+    for write in writes:
+        write.wait()
 
 
 def publish(*arrays):
@@ -504,7 +484,7 @@
         out_shape=[jax.ShapeDtypeStruct(a.shape, a.dtype) for a in arrays],
         in_specs=[spec] * len(arrays),
         out_specs=[spec] * len(arrays),
-        scratch_shapes=[pltpu.SemaphoreType.DMA((len(arrays),))],
+        scratch_shapes=[pltpu.VMEM(a.shape, a.dtype) for a in arrays] + [pltpu.SemaphoreType.DMA((2, len(arrays)))],
         name="publish",
     )(*arrays)
 

time: 116 us -> 76 us (0.66)
  Pallas kernels: 115 us -> 75 us
    pallas_call x1, Pallas kernels: 40.8 us -> 2.14 us  [publish(): pl.pallas_call(functools.partial(publish_kernel, len(arrays)), out_shape=...]
    pallas_call x1, Pallas kernels: 44 us -> 42.7 us  [attention(): pl.pallas_call(functools.partial(attention_kernel, spaces, reps), out_sha...]
where the time goes in v3:
time: 76 us; the launch traced here: 75.8 us
  Pallas kernels  75 us (99%)
  between operations  0.81 us (1%)
    pallas_call x1, Pallas kernels, attention(): pl.pallas_call(functools.partial(attention_kernel, spaces, reps), out_sha...  42.7 us
    pallas_call x1, Pallas kernels, front(): pl.pallas_call(functools.partial(front_kernel, spaces, cap), out_shape=[j...  30.1 us
    pallas_call x1, Pallas kernels, publish(): pl.pallas_call(functools.partial(publish_kernel, len(arrays)), out_shape=...  2.14 us

profile of v3, /device:TPU:1, one launch (start us, length us, event | category | flops | bytes accessed | tf_op | source)
XLA Modules:
  0.0 75.8 jit_solution(4025242282832933445)
XLA Ops:
  0.6 30.1 %front.1 = (bf16[1024,256]{1,0:T(8,128)(2,1)}, bf16[1024,256]{1,0:T(8,128)(2,1)}) custom-call(bf16[1024,256]{1,0:T(8,128)(2,1)} %bitcast.5, s32[2,26]{1,0:T(2,128)} %bitcast.9, s32[1,1024]{1,0:T(1,128)} %order.1, bf16[27,256,256]{2,1,0:T(8,128)(2,1)} %w_hbm.1), custom_call_target="tpu_custom_call" | custom-call | flops 3623878656 | bytes 5111808 | tf_op jit(solution)/shard_map/front/pallas_call | solution.py:250
  30.7 42.7 %attention.1 = (bf16[1024,256]{1,0:T(8,128)(2,1)}, f32[256,256]{1,0:T(8,128)}) custom-call(bf16[1024,256]{1,0:T(8,128)(2,1)} %get-tuple-element.11.reg, bf16[256,768]{1,0:T(8,128)(2,1)} %wi.1, bf16[256,256]{1,0:T(8,128)(2,1)} %wo.1, bf16[1024,256]{1,0:T(8,128)(2,1)} %bitcast.6), custom_call_target="tpu_custom_call" | custom-call | flops 17179869184 | bytes 2097152 | tf_op jit(solution)/shard_map/attention/pallas_call | solution.py:432
  73.5 2.1 %publish.1 = (bf16[1024,256]{1,0:T(8,128)(2,1)}, bf16[1024,256]{1,0:T(8,128)(2,1)}, f32[256,256]{1,0:T(8,128)}) custom-call(bf16[1024,256]{1,0:T(8,128)(2,1)} %get-tuple-element.10.refs_0_, bf16[1024,256]{1,0:T(8,128)(2,1)} %get-tuple-element.12.refs_1_, f32[256,256]{1,0:T(8,128)} %get-tuple-element.13.refs_2_), custom_call_target="tpu_custom_call" | custom-call | tf_op jit(solution)/shard_map/publish/pallas_call | solution.py:482

commit v4 on v3

--- a/solution.py
+++ b/solution.py
@@ -31,9 +31,9 @@
     return jnp.where(mask, 1.0, 0.0).astype(BF16)
 
 
-def front_kernel(
-    spaces, cap, feat, nb, order, w_hbm, enc, reg,
-    w, x, halo_l, halo_r, table, got, send, recv, place,
+def front_body(
+    spaces, reps, cap, feat, nb, order, w_hbm, enc_out, enc, reg, enc_sem, loads,
+    w, x, halo_l, halo_r, table, got, send, recv, place, picks, held,
     w_sem, hs, hr, ts, tr, rs, rr,
 ):
     me = lax.axis_index("space")
@@ -43,6 +43,8 @@
     bricks = rows // brick
     load = pltpu.make_async_copy(w_hbm, w, w_sem)
     load.start()
+    for later in loads:
+        later.start()
 
     def peer(k):
         return {"space": lax.rem(me + k, spaces)}
@@ -54,6 +56,11 @@
         return carry
 
     lax.fori_loop(1, spaces, greet, 0)
+    rep = lax.axis_index("rep")
+    for m in range(1, reps):
+        for core in range(2):
+            device = {"space": me // 2 * 2 + core, "rep": lax.rem(rep + m, reps)}
+            pl.semaphore_signal(barrier, inc=1, device_id=device, device_id_type=MESH)
 
     depth = iota((EDGE + 2, EDGE, width), 1)
 
@@ -127,7 +134,7 @@
     table[...] = jnp.broadcast_to(slots[:, None, :], table.shape)
     row_at = ahead.astype(F32) * float(cap) + rank
 
-    pl.semaphore_wait(barrier, spaces - 1)
+    pl.semaphore_wait(barrier, spaces - 1 + 2 * (reps - 1))
 
     halos = []
     for b in range(bricks):
@@ -160,24 +167,22 @@
 
     lax.fori_loop(1, spaces, start_table, 0)
 
-    def window(first, count, p):
-        return pl.ds(first + p * face if isinstance(first, int) else pl.multiple_of(first + p * face, face), count)
-
-    def products(p, rows_in):
-        return dot(rows_in, w[9 * p : 9 * p + 9].reshape(9 * width, width))
-
     load.wait()
-    middle = brick - 2 * face
-
-    def conv_middle(b, carry):
-        acc = jnp.zeros((middle, width), F32)
-        for p in range(3):
-            acc = acc + products(p, x[b, window(face, middle, p), :])
-        at = pl.ds(pl.multiple_of(b * brick + face, face), middle)
-        enc[at] = (feat[at].astype(F32) + acc).astype(BF16)
-        return carry
-
-    lax.fori_loop(0, bricks, conv_middle, 0)
+    tile = brick // 2
+    group = 8
+
+    def product(n, p):
+        b, half = n // 2, n % 2
+        first = pl.multiple_of(half * tile + p * face, face)
+        return dot(x[b, pl.ds(first, tile), :], w[pl.ds(9 * p, 9)].reshape(9 * width, width))
+
+    def conv_first(n, carry):
+        held[n] = product(n, 1) + product(n, 2 - 2 * (n % 2))
+        wanted = (iota((group * cap, rows), 0) + n * group * cap).astype(F32)
+        picks[pl.ds(pl.multiple_of(n * group * cap, 128), group * cap)] = onehot(wanted == row_at)
+        return carry
+
+    lax.fori_loop(0, spaces // group, conv_first, 0)
     for copy in halos:
         copy.wait_recv()
     tops = [layer(feat, n * brick + brick - face) for n in range(bricks)]
@@ -188,18 +193,16 @@
         write_layer(b, 0, -1, lefts + tops, left_ids + own_ids, None)
         write_layer(b, EDGE + 1, 1, bottoms + rights, own_ids + right_ids, None)
 
-    ends = [(b, first) for b in range(bricks) for first in (0, brick - face)]
-    acc = jnp.zeros((len(ends) * face, width), F32)
-    for p in range(3):
-        acc = acc + products(p, jnp.concatenate([x[b, window(first, face, p), :] for b, first in ends], axis=0))
-    for n, (b, first) in enumerate(ends):
-        at = pl.ds(b * brick + first, face)
-        enc[at] = (feat[at].astype(F32) + acc[n * face : (n + 1) * face]).astype(BF16)
-
-    group = 8
+    def conv_last(n, carry):
+        at = pl.ds(pl.multiple_of(n * tile, tile), tile)
+        enc[at] = (feat[at].astype(F32) + held[n] + product(n, 2 * (n % 2))).astype(BF16)
+        return carry
+
+    lax.fori_loop(0, rows // tile, conv_last, 0)
+    pltpu.make_async_copy(enc, enc_out, enc_sem).start()
+
     for c in range(spaces // group):
-        wanted = (iota((group * cap, rows), 0) + c * group * cap).astype(F32)
-        block = dot(onehot(wanted == row_at), enc[...]).astype(BF16)
+        block = dot(picks[c * group * cap : (c + 1) * group * cap], enc[...]).astype(BF16)
         send[c * group : (c + 1) * group] = block.reshape(group, cap, width)
         for k in range(max(1, c * group), (c + 1) * group):
             row_copy(k).start()
@@ -240,46 +243,8 @@
         copy.wait_send()
 
 
-def front(features, neighbours, order, weight):
-    spaces = lax.axis_size("space")
-    rows, width = features.shape
-    cap = 3 * rows // (2 * spaces)
-    bricks = rows // EDGE**3
-    face = EDGE * EDGE
-    vmem = pl.BlockSpec(memory_space=pltpu.VMEM)
-    return pl.pallas_call(
-        functools.partial(front_kernel, spaces, cap),
-        out_shape=[jax.ShapeDtypeStruct((rows, width), BF16)] * 2,
-        in_specs=[vmem, pl.BlockSpec(memory_space=pltpu.SMEM), vmem, pl.BlockSpec(memory_space=pl.ANY)],
-        out_specs=[vmem, vmem],
-        scratch_shapes=[
-            pltpu.VMEM(weight.shape, BF16),
-            pltpu.VMEM((bricks, (EDGE + 2) * face, 9 * width), BF16),
-            pltpu.VMEM((bricks, face, width), BF16),
-            pltpu.VMEM((bricks, face, width), BF16),
-            pltpu.VMEM((spaces, 8, 128), F32),
-            pltpu.VMEM((spaces, 8, 128), F32),
-            pltpu.VMEM((spaces, cap, width), BF16),
-            pltpu.VMEM((spaces, cap, width), BF16),
-            pltpu.VMEM((rows, spaces * cap), BF16),
-            pltpu.SemaphoreType.DMA,
-            pltpu.SemaphoreType.DMA((2 * bricks,)),
-            pltpu.SemaphoreType.DMA((2 * bricks,)),
-            pltpu.SemaphoreType.DMA((spaces,)),
-            pltpu.SemaphoreType.DMA((spaces,)),
-            pltpu.SemaphoreType.DMA((spaces,)),
-            pltpu.SemaphoreType.DMA((spaces,)),
-        ],
-        compiler_params=pltpu.CompilerParams(collective_id=0, has_side_effects=True, vmem_limit_bytes=VMEM_LIMIT),
-        cost_estimate=pl.CostEstimate(
-            flops=2 * rows * 27 * width * width, bytes_accessed=weight.size * 2 + 6 * rows * width, transcendentals=0
-        ),
-        name="front",
-    )(features, neighbours, order, weight)
-
-
-def attention_kernel(
-    spaces, reps, reg, wi, wo, cot, att, grad,
+def attention_body(
+    spaces, reps, reg, wi, wo, cot, att_out, att, grad, loads, att_sem,
     q, k, v, ctx, s0, s1, *comm,
 ):
     chunks = [comm[n : n + 11] for n in range(0, len(comm), 11)]
@@ -305,10 +270,6 @@
 
         lax.fori_loop(1, count, body, 0)
 
-    barrier = pltpu.get_barrier_semaphore()
-    run(planes, lambda n: pl.semaphore_signal(barrier, inc=1, device_id=across(n), device_id_type=MESH))
-    run(others, lambda n: pl.semaphore_signal(barrier, inc=1, device_id=along(n), device_id_type=MESH))
-
     def copy(src, dst, send, recv, device):
         return pltpu.make_async_remote_copy(
             src_ref=src, dst_ref=dst, send_sem=send, recv_sem=recv, device_id=device, device_id_type=MESH
@@ -355,6 +316,8 @@
         part_context = ctx[side].astype(BF16)
         return lax.dot_general(part_context, cot[...], (((0,), (0,)), ((), ())), preferred_element_type=F32)
 
+    for load in loads:
+        load.wait()
     residual = reg[...].astype(F32)
     centred = residual - jnp.mean(residual, axis=-1, keepdims=True)
     variance = jnp.mean(centred * centred, axis=-1, keepdims=True)
@@ -396,9 +359,7 @@
 
         @pl.when(n == 1)
         def _():
-            values = gradient_rows(0)
-            pl.semaphore_wait(barrier, planes + others - 2)
-            start_scatter(0, values)
+            start_scatter(0, gradient_rows(0))
 
         @pl.when(n == 2)
         def _():
@@ -413,6 +374,7 @@
     start_gather(0)
     context = jnp.concatenate([ctx[0], ctx[1]], axis=1).astype(BF16)
     att[...] = (reg[...].astype(F32) + dot(context, wo[...])).astype(BF16)
+    pltpu.make_async_copy(att, att_out, att_sem).start()
     start_share(2)
     start_gather(1)
     finish(0, slice(0, half))
@@ -421,47 +383,97 @@
     finish(2, slice(half + half // 2, width))
 
 
-def attention(regrouped, wi, wo, cot):
+def layer_kernel(spaces, reps, cap, feat, nb, order, *refs):
+    w_hbm, wi_hbm, wo_hbm, cot_hbm, enc_out, att_out, grad_out = refs[:7]
+    wi, wo, cot, enc, reg, att, grad, sems = refs[7:15]
+    front_refs, attention_refs = refs[15:33], refs[33:]
+    loads = [
+        pltpu.make_async_copy(source, held, sems.at[n])
+        for n, (source, held) in enumerate(((wi_hbm, wi), (wo_hbm, wo), (cot_hbm, cot)))
+    ]
+    front_body(spaces, reps, cap, feat, nb, order, w_hbm, enc_out, enc, reg, sems.at[3], loads, *front_refs)
+    attention_body(spaces, reps, reg, wi, wo, cot, att_out, att, grad, loads, sems.at[4], *attention_refs)
+    last = pltpu.make_async_copy(grad, grad_out, sems.at[5])
+    last.start()
+    pltpu.make_async_copy(enc, enc_out, sems.at[3]).wait()
+    pltpu.make_async_copy(att, att_out, sems.at[4]).wait()
+    last.wait()
+
+
+def layer(features, neighbours, order, weight, wi, wo, cot):
     spaces, reps = lax.axis_size("space"), lax.axis_size("rep")
-    rows, width = regrouped.shape
+    rows, width = features.shape
+    cap = 3 * rows // (2 * spaces)
+    bricks = rows // EDGE**3
+    face = EDGE * EDGE
     half = width // 2
     planes, others = spaces // 2, 2 * reps
     tile = 256
     vmem = pl.BlockSpec(memory_space=pltpu.VMEM)
+    hbm = pl.BlockSpec(memory_space=pl.ANY)
     dma = pltpu.SemaphoreType.DMA
+    full = pltpu.VMEM((rows, width), BF16)
+    shared = [
+        pltpu.VMEM(wi.shape, BF16),
+        pltpu.VMEM(wo.shape, BF16),
+        *[full] * 4,
+        pltpu.VMEM((width, width), F32),
+        dma((6,)),
+    ]
+    for_front = [
+        pltpu.VMEM(weight.shape, BF16),
+        pltpu.VMEM((bricks, (EDGE + 2) * face, 9 * width), BF16),
+        pltpu.VMEM((bricks, face, width), BF16),
+        pltpu.VMEM((bricks, face, width), BF16),
+        pltpu.VMEM((spaces, 8, 128), F32),
+        pltpu.VMEM((spaces, 8, 128), F32),
+        pltpu.VMEM((spaces, cap, width), BF16),
+        pltpu.VMEM((spaces, cap, width), BF16),
+        pltpu.VMEM((rows, spaces * cap), BF16),
+        pltpu.VMEM((spaces * cap, rows), BF16),
+        pltpu.VMEM((2 * bricks, EDGE**3 // 2, width), F32),
+        dma,
+        dma((2 * bricks,)),
+        dma((2 * bricks,)),
+        *[dma((spaces,))] * 4,
+    ]
+    for_attention = [
+        full,
+        full,
+        pltpu.VMEM((2, rows, width), BF16),
+        pltpu.VMEM((2, rows, half), F32),
+        pltpu.VMEM((tile, rows), F32),
+        pltpu.VMEM((tile, rows), F32),
+    ]
+    for count in (half, half // 2, half // 2):
+        for_attention += [
+            pltpu.VMEM((others, count // others, width), F32),
+            pltpu.VMEM((others, count // others, width), F32),
+            pltpu.VMEM((count // others, width), F32),
+            pltpu.VMEM((planes, count // others, width), F32),
+            pltpu.VMEM((others, count // others, width), F32),
+            *[dma((others,))] * 2,
+            *[dma((planes,))] * 2,
+            *[dma((others,))] * 2,
+        ]
     return pl.pallas_call(
-        functools.partial(attention_kernel, spaces, reps),
-        out_shape=[jax.ShapeDtypeStruct((rows, width), BF16), jax.ShapeDtypeStruct((width, width), F32)],
-        in_specs=[vmem] * 4,
-        out_specs=[vmem, vmem],
-        scratch_shapes=[
-            pltpu.VMEM((rows, width), BF16),
-            pltpu.VMEM((rows, width), BF16),
-            pltpu.VMEM((2, rows, width), BF16),
-            pltpu.VMEM((2, rows, half), F32),
-            pltpu.VMEM((tile, rows), F32),
-            pltpu.VMEM((tile, rows), F32),
-        ]
-        + [
-            spec
-            for count in (half, half // 2, half // 2)
-            for spec in (
-                pltpu.VMEM((others, count // others, width), F32),
-                pltpu.VMEM((others, count // others, width), F32),
-                pltpu.VMEM((count // others, width), F32),
-                pltpu.VMEM((planes, count // others, width), F32),
-                pltpu.VMEM((others, count // others, width), F32),
-                *[dma((others,))] * 2,
-                *[dma((planes,))] * 2,
-                *[dma((others,))] * 2,
-            )
+        functools.partial(layer_kernel, spaces, reps, cap),
+        out_shape=[
+            jax.ShapeDtypeStruct((rows, width), BF16),
+            jax.ShapeDtypeStruct((rows, width), BF16),
+            jax.ShapeDtypeStruct((width, width), F32),
         ],
-        compiler_params=pltpu.CompilerParams(collective_id=1, has_side_effects=True, vmem_limit_bytes=VMEM_LIMIT),
+        in_specs=[vmem, pl.BlockSpec(memory_space=pltpu.SMEM), vmem, hbm, hbm, hbm, hbm],
+        out_specs=[hbm] * 3,
+        scratch_shapes=shared + for_front + for_attention,
+        compiler_params=pltpu.CompilerParams(collective_id=0, has_side_effects=True, vmem_limit_bytes=VMEM_LIMIT),
         cost_estimate=pl.CostEstimate(
-            flops=4 * HEADS * rows * rows * width, bytes_accessed=8 * rows * width, transcendentals=HEADS * rows * rows
+            flops=2 * rows * 27 * width * width + 4 * HEADS * rows * rows * width,
+            bytes_accessed=weight.size * 2 + 12 * rows * width,
+            transcendentals=HEADS * rows * rows,
         ),
-        name="attention",
-    )(regrouped, wi, wo, cot)
+        name="layer",
+    )(features, neighbours, order, weight, wi, wo, cot)
 
 
 def publish_kernel(count, *refs):
@@ -490,9 +502,10 @@
 
 
 def local(features, neighbours, serial_order, kernel_weight, input_projection, output_projection, cotangent):
-    encoded, regrouped = front(features[0], neighbours[0], serial_order, kernel_weight)
-    attended, gradient = attention(regrouped, input_projection, output_projection, cotangent[0])
-    encoded, attended, gradient = publish(encoded, attended, gradient)
+    results = layer(
+        features[0], neighbours[0], serial_order, kernel_weight, input_projection, output_projection, cotangent[0]
+    )
+    encoded, attended, gradient = publish(*results)
     return encoded[None], attended[None], gradient
 
 

time: 76 us -> 75.1 us (0.988)
  Pallas kernels: 75 us -> 74.2 us
    pallas_call x2 -> x1, Pallas kernels: 72.8 us -> 72 us  [layer(): pl.pallas_call(functools.partial(layer_kernel, spaces, reps, cap), out_sh...]
where the time goes in v4:
time: 75.1 us; the launch traced here: 75 us
  Pallas kernels  74.2 us (99%)
  between operations  0.8 us (1%)
    pallas_call x1, Pallas kernels, layer(): pl.pallas_call(functools.partial(layer_kernel, spaces, reps, cap), out_sh...  72 us
    pallas_call x1, Pallas kernels, publish(): pl.pallas_call(functools.partial(publish_kernel, len(arrays)), out_shape=...  2.14 us

profile of v4, /device:TPU:1, one launch (start us, length us, event | category | flops | bytes accessed | tf_op | source)
XLA Modules:
  0.0 75.0 jit_solution(13926889323565434390)
XLA Ops:
  0.6 72.0 %layer.1 = (bf16[1024,256]{1,0:T(8,128)(2,1)}, bf16[1024,256]{1,0:T(8,128)(2,1)}, f32[256,256]{1,0:T(8,128)}) custom-call(bf16[1024,256]{1,0:T(8,128)(2,1)} %bitcast.5, s32[2,26]{1,0:T(2,128)} %bitcast.9, s32[1,1024]{1,0:T(1,128)} %order.1, bf16[27,256,256]{2,1,0:T(8,128)(2,1)} %refs_0_.1, bf16[256,768]{1,0:T(8,128)(2,1)} %refs_1_.1, ...), custom_call_target="tpu_custom_call" | custom-call | flops 20803747840 | bytes 6684672 | tf_op jit(solution)/shard_map/layer/pallas_call | solution.py:459
  72.7 2.1 %publish.1 = (bf16[1024,256]{1,0:T(8,128)(2,1)}, bf16[1024,256]{1,0:T(8,128)(2,1)}, f32[256,256]{1,0:T(8,128)}) custom-call(bf16[1024,256]{1,0:T(8,128)(2,1)} %get-tuple-element.9.refs_0_, bf16[1024,256]{1,0:T(8,128)(2,1)} %get-tuple-element.10.refs_1_, f32[256,256]{1,0:T(8,128)} %get-tuple-element.11.refs_2_), custom_call_target="tpu_custom_call" | custom-call | tf_op jit(solution)/shard_map/publish/pallas_call | solution.py:494

commit v5 on v4

--- a/solution.py
+++ b/solution.py
@@ -32,15 +32,17 @@
 
 
 def front_body(
-    spaces, reps, cap, feat, nb, order, w_hbm, enc_out, enc, reg, enc_sem, loads,
-    w, x, halo_l, halo_r, table, got, send, recv, place, picks, held,
-    w_sem, hs, hr, ts, tr, rs, rr,
+    spaces, reps, cap, feat, nb, order, w_hbm, enc_out, enc, reg, enc_sem, loads, meanwhile,
+    w, x, halo_l, halo_r, table, passed, got, send, recv, place, picks, held,
+    w_sem, hs, hr, ts, tr, us, ur, rs, rr,
 ):
     me = lax.axis_index("space")
     rows, width = feat.shape
     face = EDGE * EDGE
     brick = EDGE * face
     bricks = rows // brick
+    outer, inner = got.shape[:2]
+    line, within = me // inner, lax.rem(me, inner)
     load = pltpu.make_async_copy(w_hbm, w, w_sem)
     load.start()
     for later in loads:
@@ -95,11 +97,12 @@
             here,
             pltpu.roll(jnp.where(depth == 0, above, here), EDGE - 1, 1),
         )
-        first = i * face if isinstance(i, int) else pl.multiple_of(i * face, face)
+        first = (i * bricks + b) * face
+        first = first if isinstance(first, int) else pl.multiple_of(first, face)
         for q in range(3):
             for r in range(3):
                 n = 3 * q + r
-                x[b, pl.ds(first, face), n * width : (n + 1) * width] = (
+                x[pl.ds(first, face), n * width : (n + 1) * width] = (
                     variants[r][q : q + EDGE].reshape(face, width).astype(BF16)
                 )
 
@@ -107,31 +110,32 @@
     left_ids = [(me - 1) * bricks + n for n in range(bricks)]
     right_ids = [(me + 1) * bricks + n for n in range(bricks)]
 
-    def inner(i, carry):
+    def inner_layer(i, carry):
         sources = [layer(feat, pl.multiple_of(n * brick + i * face, face)) for n in range(bricks)]
         for b in range(bricks):
             write_layer(b, i + 1, 0, sources, own_ids, sources[b])
         return carry
 
-    lax.fori_loop(0, EDGE, inner, 0)
+    lax.fori_loop(0, EDGE, inner_layer, 0)
 
     places = order[...]
     shift = rows.bit_length() - 1
     owner = lax.shift_right_logical(places, shift)
     slot = places & (rows - 1)
     ahead = (owner - me + spaces) & (spaces - 1)
-    chosen = jnp.where(iota((spaces, rows), 0) == ahead, 1.0, 0.0)
+    chosen = jnp.where(iota((spaces, rows), 0) == owner, 1.0, 0.0)
     before = onehot(iota((rows, rows), 0) < iota((rows, rows), 1))
     rank = jnp.sum(chosen * dot(chosen.astype(BF16), before), axis=0, keepdims=True)
     high = lax.shift_right_logical(slot, 5).astype(F32)
     low = (slot & 31).astype(F32)
-    lanes = table.shape[2]
+    lanes = table.shape[3]
     by_rank = onehot(iota((lanes, rows), 0).astype(F32) == rank)
     stacked = jnp.concatenate([chosen * high, chosen * low, chosen], axis=0).astype(BF16)
     found = dot_t(stacked, by_rank)
     slots = found[:spaces] * 32.0 + found[spaces : 2 * spaces]
     slots = jnp.where(found[2 * spaces :] > 0.5, slots, -1.0)
-    table[...] = jnp.broadcast_to(slots[:, None, :], table.shape)
+    for n in range(outer):
+        table[:, n] = jnp.broadcast_to(slots[n * inner : (n + 1) * inner][:, None, :], (inner, 8, lanes))
     row_at = ahead.astype(F32) * float(cap) + rank
 
     pl.semaphore_wait(barrier, spaces - 1 + 2 * (reps - 1))
@@ -149,10 +153,17 @@
             copy.start()
             halos.append(copy)
 
-    def table_copy(k):
+    def inner_table(n, sender):
         return pltpu.make_async_remote_copy(
-            src_ref=table.at[k], dst_ref=got.at[k], send_sem=ts.at[k], recv_sem=tr.at[k],
-            device_id=peer(k), device_id_type=MESH,
+            src_ref=table.at[lax.rem(within + n, inner)], dst_ref=passed.at[sender], send_sem=ts.at[n], recv_sem=tr.at[n],
+            device_id={"space": line * inner + lax.rem(within + n, inner)}, device_id_type=MESH,
+        )
+
+    def outer_table(n, sender):
+        there = lax.rem(line + n, outer)
+        return pltpu.make_async_remote_copy(
+            src_ref=passed.at[:, there], dst_ref=got.at[sender], send_sem=us.at[n], recv_sem=ur.at[n],
+            device_id={"space": there * inner + within}, device_id_type=MESH,
         )
 
     def row_copy(k):
@@ -161,28 +172,32 @@
             device_id=peer(k), device_id_type=MESH,
         )
 
-    def start_table(k, carry):
-        table_copy(k).start()
+    for n in range(1, inner):
+        inner_table(n, within).start()
+
+    load.wait()
+    halves = EDGE // 2
+    block = halves * bricks * face
+    group = 8
+
+    def product(n, p):
+        first = pl.multiple_of((n * halves + p) * bricks * face, face)
+        return dot(x[pl.ds(first, block), :], w[pl.ds(9 * p, 9)].reshape(9 * width, width))
+
+    def conv_first(n, carry):
+        held[n] = product(n, 1) + product(n, 2 - 2 * n)
+        part = spaces * cap // 2
+        wanted = (iota((part, rows), 0) + n * part).astype(F32)
+        picks[pl.ds(pl.multiple_of(n * part, 128), part)] = onehot(wanted == row_at)
         return carry
 
-    lax.fori_loop(1, spaces, start_table, 0)
-
-    load.wait()
-    tile = brick // 2
-    group = 8
-
-    def product(n, p):
-        b, half = n // 2, n % 2
-        first = pl.multiple_of(half * tile + p * face, face)
-        return dot(x[b, pl.ds(first, tile), :], w[pl.ds(9 * p, 9)].reshape(9 * width, width))
-
-    def conv_first(n, carry):
-        held[n] = product(n, 1) + product(n, 2 - 2 * (n % 2))
-        wanted = (iota((group * cap, rows), 0) + n * group * cap).astype(F32)
-        picks[pl.ds(pl.multiple_of(n * group * cap, 128), group * cap)] = onehot(wanted == row_at)
-        return carry
-
-    lax.fori_loop(0, spaces // group, conv_first, 0)
+    lax.fori_loop(0, 2, conv_first, 0)
+    passed[within] = table[within]
+    for n in range(1, inner):
+        inner_table(n, within).wait_send()
+        inner_table(n, lax.rem(within - n + inner, inner)).wait_recv()
+    for n in range(1, outer):
+        outer_table(n, line).start()
     for copy in halos:
         copy.wait_recv()
     tops = [layer(feat, n * brick + brick - face) for n in range(bricks)]
@@ -194,11 +209,15 @@
         write_layer(b, EDGE + 1, 1, bottoms + rights, own_ids + right_ids, None)
 
     def conv_last(n, carry):
-        at = pl.ds(pl.multiple_of(n * tile, tile), tile)
-        enc[at] = (feat[at].astype(F32) + held[n] + product(n, 2 * (n % 2))).astype(BF16)
+        total = held[n] + product(n, 2 * n)
+        for i in range(halves):
+            for b in range(bricks):
+                at = pl.ds(pl.multiple_of(b * brick + (n * halves + i) * face, face), face)
+                rows_in = (i * bricks + b) * face
+                enc[at] = (feat[at].astype(F32) + total[rows_in : rows_in + face]).astype(BF16)
         return carry
 
-    lax.fori_loop(0, rows // tile, conv_last, 0)
+    lax.fori_loop(0, 2, conv_last, 0)
     pltpu.make_async_copy(enc, enc_out, enc_sem).start()
 
     for c in range(spaces // group):
@@ -207,13 +226,12 @@
         for k in range(max(1, c * group), (c + 1) * group):
             row_copy(k).start()
     recv[0] = send[0]
-    got[0] = table[0]
-
-    def wait_table(k, carry):
-        table_copy(k).wait()
-        return carry
-
-    lax.fori_loop(1, spaces, wait_table, 0)
+    meanwhile()
+    for n in range(inner):
+        got[line, n] = passed[n, line]
+    for n in range(1, outer):
+        outer_table(n, line).wait_send()
+        outer_table(n, lax.rem(line - n + outer, outer)).wait_recv()
     column = iota((8, 128), 1)
     for t in range(spaces * cap // 128):
         lane = jnp.full((8, 128), -1.0, F32)
@@ -221,7 +239,8 @@
             start, end = max(0, k * cap - 128 * t), min(128, (k + 1) * cap - 128 * t)
             if start >= end:
                 continue
-            moved = got[k]
+            source = lax.rem(me - k + spaces, spaces)
+            moved = got[source // inner, lax.rem(source, inner)]
             if (k * cap - 128 * t) % 128:
                 moved = pltpu.roll(moved, (k * cap - 128 * t) % 128, 1)
             lane = jnp.where((column >= start) & (column < end), moved, lane)
@@ -325,10 +344,8 @@
     packed = dot(normed, wi[...]).astype(BF16)
     q[...] = packed[:, :width] * jnp.asarray(head**-0.5, BF16)
     k[...] = packed[:, width : 2 * width]
-    ones = jnp.ones((rows, half), BF16)
     for n in range(2):
-        v[n] = jnp.concatenate([packed[:, 2 * width + n * half : 2 * width + (n + 1) * half], ones], axis=1)
-    ctx[...] = jnp.zeros_like(ctx)
+        v[n, :, :half] = packed[:, 2 * width + n * half : 2 * width + (n + 1) * half]
     tile = s0.shape[0]
     tiles = rows // tile
     lane_q = iota((tile, width), 1) // head
@@ -386,12 +403,18 @@
 def layer_kernel(spaces, reps, cap, feat, nb, order, *refs):
     w_hbm, wi_hbm, wo_hbm, cot_hbm, enc_out, att_out, grad_out = refs[:7]
     wi, wo, cot, enc, reg, att, grad, sems = refs[7:15]
-    front_refs, attention_refs = refs[15:33], refs[33:]
+    front_refs, attention_refs = refs[15:36], refs[36:]
+    v, ctx = attention_refs[2:4]
     loads = [
         pltpu.make_async_copy(source, held, sems.at[n])
         for n, (source, held) in enumerate(((wi_hbm, wi), (wo_hbm, wo), (cot_hbm, cot)))
     ]
-    front_body(spaces, reps, cap, feat, nb, order, w_hbm, enc_out, enc, reg, sems.at[3], loads, *front_refs)
+
+    def meanwhile():
+        v[:, :, ctx.shape[2] :] = jnp.ones(ctx.shape, BF16)
+        ctx[...] = jnp.zeros_like(ctx)
+
+    front_body(spaces, reps, cap, feat, nb, order, w_hbm, enc_out, enc, reg, sems.at[3], loads, meanwhile, *front_refs)
     attention_body(spaces, reps, reg, wi, wo, cot, att_out, att, grad, loads, sems.at[4], *attention_refs)
     last = pltpu.make_async_copy(grad, grad_out, sems.at[5])
     last.start()
@@ -407,6 +430,7 @@
     bricks = rows // EDGE**3
     face = EDGE * EDGE
     half = width // 2
+    inner, outer = 8, spaces // 8
     planes, others = spaces // 2, 2 * reps
     tile = 256
     vmem = pl.BlockSpec(memory_space=pltpu.VMEM)
@@ -422,20 +446,23 @@
     ]
     for_front = [
         pltpu.VMEM(weight.shape, BF16),
-        pltpu.VMEM((bricks, (EDGE + 2) * face, 9 * width), BF16),
+        pltpu.VMEM(((EDGE + 2) * bricks * face, 9 * width), BF16),
         pltpu.VMEM((bricks, face, width), BF16),
         pltpu.VMEM((bricks, face, width), BF16),
-        pltpu.VMEM((spaces, 8, 128), F32),
-        pltpu.VMEM((spaces, 8, 128), F32),
+        pltpu.VMEM((inner, outer, 8, 128), F32),
+        pltpu.VMEM((inner, outer, 8, 128), F32),
+        pltpu.VMEM((outer, inner, 8, 128), F32),
         pltpu.VMEM((spaces, cap, width), BF16),
         pltpu.VMEM((spaces, cap, width), BF16),
         pltpu.VMEM((rows, spaces * cap), BF16),
         pltpu.VMEM((spaces * cap, rows), BF16),
-        pltpu.VMEM((2 * bricks, EDGE**3 // 2, width), F32),
+        pltpu.VMEM((2, rows // 2, width), F32),
         dma,
         dma((2 * bricks,)),
         dma((2 * bricks,)),
-        *[dma((spaces,))] * 4,
+        *[dma((inner,))] * 2,
+        *[dma((outer,))] * 2,
+        *[dma((spaces,))] * 2,
     ]
     for_attention = [
         full,

time: 75.1 us -> 74.3 us (0.989)
  Pallas kernels: 74.2 us -> 73.3 us
    pallas_call x1, Pallas kernels: 72 us -> 71.2 us  [layer(): pl.pallas_call(functools.partial(layer_kernel, spaces, reps, cap), out_sh...]
where the time goes in v5:
time: 74.3 us; the launch traced here: 74.1 us
  Pallas kernels  73.3 us (99%)
  between operations  0.8 us (1%)
    pallas_call x1, Pallas kernels, layer(): pl.pallas_call(functools.partial(layer_kernel, spaces, reps, cap), out_sh...  71.2 us
    pallas_call x1, Pallas kernels, publish(): pl.pallas_call(functools.partial(publish_kernel, len(arrays)), out_shape=...  2.14 us

profile of v5, /device:TPU:1, one launch (start us, length us, event | category | flops | bytes accessed | tf_op | source)
XLA Modules:
  0.0 74.1 jit_solution(7430911475034604996)
XLA Ops:
  0.6 71.2 %layer.1 = (bf16[1024,256]{1,0:T(8,128)(2,1)}, bf16[1024,256]{1,0:T(8,128)(2,1)}, f32[256,256]{1,0:T(8,128)}) custom-call(bf16[1024,256]{1,0:T(8,128)(2,1)} %bitcast.5, s32[2,26]{1,0:T(2,128)} %bitcast.9, s32[1,1024]{1,0:T(1,128)} %order.1, bf16[27,256,256]{2,1,0:T(8,128)(2,1)} %refs_0_.1, bf16[256,768]{1,0:T(8,128)(2,1)} %refs_1_.1, ...), custom_call_target="tpu_custom_call" | custom-call | flops 20803747840 | bytes 6684672 | tf_op jit(solution)/shard_map/layer/pallas_call | solution.py:486
  71.8 2.1 %publish.1 = (bf16[1024,256]{1,0:T(8,128)(2,1)}, bf16[1024,256]{1,0:T(8,128)(2,1)}, f32[256,256]{1,0:T(8,128)}) custom-call(bf16[1024,256]{1,0:T(8,128)(2,1)} %get-tuple-element.9.refs_0_, bf16[1024,256]{1,0:T(8,128)(2,1)} %get-tuple-element.10.refs_1_, f32[256,256]{1,0:T(8,128)} %get-tuple-element.11.refs_2_), custom_call_target="tpu_custom_call" | custom-call | tf_op jit(solution)/shard_map/publish/pallas_call | solution.py:521

commit v6 on v5

--- a/solution.py
+++ b/solution.py
@@ -1,4 +1,5 @@
 import functools
+import math
 
 import jax
 import jax.numpy as jnp
@@ -263,7 +264,7 @@
 
 
 def attention_body(
-    spaces, reps, reg, wi, wo, cot, att_out, att, grad, loads, att_sem,
+    spaces, reps, reg, wi, wo, cot, att_out, att, grad_out, grad, loads, att_sem, grad_sems,
     q, k, v, ctx, s0, s1, *comm,
 ):
     chunks = [comm[n : n + 11] for n in range(0, len(comm), 11)]
@@ -275,6 +276,9 @@
     chip, core = space // 2, space % 2
     place = rep * 2 + core
 
+    side = math.isqrt(planes)
+    far_first = sorted(range(1, planes), key=lambda n: -sum(min(d, side - d) for d in (n // side, n % side)))
+
     def across(n):
         return {"space": lax.rem(chip + n, planes) * 2 + core}
 
@@ -315,7 +319,8 @@
         first[0] = term[place]
         run(others, lambda n: scatter(c, n).wait())
         part[...] = jnp.sum(first[...], axis=0)
-        run(planes, lambda n: share(c, n, chip).start())
+        for n in far_first:
+            share(c, n, chip).start()
 
     def start_gather(c):
         part, second, final = chunks[c][2:5]
@@ -330,6 +335,7 @@
         run(others, lambda n: gather(c, n, place).wait_send())
         run(others, lambda n: gather(c, n, lax.rem(place - n + others, others)).wait_recv())
         grad[at] = final[...].reshape(-1, width)
+        pltpu.make_async_copy(grad.at[at], grad_out.at[at], grad_sems.at[c]).start()
 
     def gradient_rows(side):
         part_context = ctx[side].astype(BF16)
@@ -388,23 +394,25 @@
     lax.fori_loop(0, 4, step, 0)
     start_scatter(2, gradient_rows(1)[half // 2 :])
     start_share(1)
-    start_gather(0)
     context = jnp.concatenate([ctx[0], ctx[1]], axis=1).astype(BF16)
     att[...] = (reg[...].astype(F32) + dot(context, wo[...])).astype(BF16)
     pltpu.make_async_copy(att, att_out, att_sem).start()
     start_share(2)
+    start_gather(0)
     start_gather(1)
-    finish(0, slice(0, half))
+    finish(0, pl.ds(0, half))
     start_gather(2)
-    finish(1, slice(half, half + half // 2))
-    finish(2, slice(half + half // 2, width))
+    finish(1, pl.ds(half, half // 2))
+    finish(2, pl.ds(half + half // 2, half // 2))
+    for c, at in enumerate((pl.ds(0, half), pl.ds(half, half // 2), pl.ds(half + half // 2, half // 2))):
+        pltpu.make_async_copy(grad.at[at], grad_out.at[at], grad_sems.at[c]).wait()
 
 
 def layer_kernel(spaces, reps, cap, feat, nb, order, *refs):
     w_hbm, wi_hbm, wo_hbm, cot_hbm, enc_out, att_out, grad_out = refs[:7]
     wi, wo, cot, enc, reg, att, grad, sems = refs[7:15]
     front_refs, attention_refs = refs[15:36], refs[36:]
-    v, ctx = attention_refs[2:4]
+    v, ctx = attention_refs[3:5]
     loads = [
         pltpu.make_async_copy(source, held, sems.at[n])
         for n, (source, held) in enumerate(((wi_hbm, wi), (wo_hbm, wo), (cot_hbm, cot)))
@@ -415,12 +423,12 @@
         ctx[...] = jnp.zeros_like(ctx)
 
     front_body(spaces, reps, cap, feat, nb, order, w_hbm, enc_out, enc, reg, sems.at[3], loads, meanwhile, *front_refs)
-    attention_body(spaces, reps, reg, wi, wo, cot, att_out, att, grad, loads, sems.at[4], *attention_refs)
-    last = pltpu.make_async_copy(grad, grad_out, sems.at[5])
-    last.start()
+    grad_sems = attention_refs[0]
+    attention_body(
+        spaces, reps, reg, wi, wo, cot, att_out, att, grad_out, grad, loads, sems.at[4], grad_sems, *attention_refs[1:]
+    )
     pltpu.make_async_copy(enc, enc_out, sems.at[3]).wait()
     pltpu.make_async_copy(att, att_out, sems.at[4]).wait()
-    last.wait()
 
 
 def layer(features, neighbours, order, weight, wi, wo, cot):
@@ -442,7 +450,7 @@
         pltpu.VMEM(wo.shape, BF16),
         *[full] * 4,
         pltpu.VMEM((width, width), F32),
-        dma((6,)),
+        dma((5,)),
     ]
     for_front = [
         pltpu.VMEM(weight.shape, BF16),
@@ -465,6 +473,7 @@
         *[dma((spaces,))] * 2,
     ]
     for_attention = [
+        dma((3,)),
         full,
         full,
         pltpu.VMEM((2, rows, width), BF16),

time: 74.3 us -> 73.6 us (level)
  no operation moved by 1% of the time
where the time goes in v6:
time: 73.6 us; the launch traced here: 73.4 us
  Pallas kernels  72.6 us (99%)
  between operations  0.8 us (1%)
    pallas_call x1, Pallas kernels, layer(): pl.pallas_call(functools.partial(layer_kernel, spaces, reps, cap), out_sh...  70.5 us
    pallas_call x1, Pallas kernels, publish(): pl.pallas_call(functools.partial(publish_kernel, len(arrays)), out_shape=...  2.14 us

profile of v6, /device:TPU:1, one launch (start us, length us, event | category | flops | bytes accessed | tf_op | source)
XLA Modules:
  0.0 73.4 jit_solution(395535449155972687)
XLA Ops:
  0.6 70.5 %layer.1 = (bf16[1024,256]{1,0:T(8,128)(2,1)}, bf16[1024,256]{1,0:T(8,128)(2,1)}, f32[256,256]{1,0:T(8,128)}) custom-call(bf16[1024,256]{1,0:T(8,128)(2,1)} %bitcast.5, s32[2,26]{1,0:T(2,128)} %bitcast.9, s32[1,1024]{1,0:T(1,128)} %order.1, bf16[27,256,256]{2,1,0:T(8,128)(2,1)} %refs_0_.1, bf16[256,768]{1,0:T(8,128)(2,1)} %refs_1_.1, ...), custom_call_target="tpu_custom_call" | custom-call | flops 20803747840 | bytes 6684672 | tf_op jit(solution)/shard_map/layer/pallas_call | solution.py:495
  71.1 2.1 %publish.1 = (bf16[1024,256]{1,0:T(8,128)(2,1)}, bf16[1024,256]{1,0:T(8,128)(2,1)}, f32[256,256]{1,0:T(8,128)}) custom-call(bf16[1024,256]{1,0:T(8,128)(2,1)} %get-tuple-element.9.refs_0_, bf16[1024,256]{1,0:T(8,128)(2,1)} %get-tuple-element.10.refs_1_, f32[256,256]{1,0:T(8,128)} %get-tuple-element.11.refs_2_), custom_call_target="tpu_custom_call" | custom-call | tf_op jit(solution)/shard_map/publish/pallas_call | solution.py:530

commit v7 on v6

--- a/solution.py
+++ b/solution.py
@@ -221,7 +221,9 @@
     lax.fori_loop(0, 2, conv_last, 0)
     pltpu.make_async_copy(enc, enc_out, enc_sem).start()
 
-    for c in range(spaces // group):
+    lines = spaces // group
+    order_of_lines = sorted(range(lines), key=lambda c: -min(c, lines - c))
+    for c in order_of_lines:
         block = dot(picks[c * group * cap : (c + 1) * group * cap], enc[...]).astype(BF16)
         send[c * group : (c + 1) * group] = block.reshape(group, cap, width)
         for k in range(max(1, c * group), (c + 1) * group):
@@ -247,7 +249,7 @@
             lane = jnp.where((column >= start) & (column < end), moved, lane)
         place[:, t * 128 : (t + 1) * 128] = onehot(iota((rows, 128), 0).astype(F32) == lane[0:1])
     total = jnp.zeros((rows, width), F32)
-    for c in range(spaces // group):
+    for c in order_of_lines:
         for k in range(max(1, c * group), (c + 1) * group):
             row_copy(k).wait_recv()
         arrived = recv[c * group : (c + 1) * group].reshape(group * cap, width)

time: 73.6 us -> 72.9 us (level)
  no operation moved by 1% of the time
where the time goes in v7:
time: 72.9 us; the launch traced here: 72.7 us
  Pallas kernels  71.9 us (99%)
  between operations  0.8 us (1%)
    pallas_call x1, Pallas kernels, layer(): pl.pallas_call(functools.partial(layer_kernel, spaces, reps, cap), out_sh...  69.8 us
    pallas_call x1, Pallas kernels, publish(): pl.pallas_call(functools.partial(publish_kernel, len(arrays)), out_shape=...  2.14 us

profile of v7, /device:TPU:1, one launch (start us, length us, event | category | flops | bytes accessed | tf_op | source)
XLA Modules:
  0.0 72.7 jit_solution(9595399769567933670)
XLA Ops:
  0.6 69.8 %layer.1 = (bf16[1024,256]{1,0:T(8,128)(2,1)}, bf16[1024,256]{1,0:T(8,128)(2,1)}, f32[256,256]{1,0:T(8,128)}) custom-call(bf16[1024,256]{1,0:T(8,128)(2,1)} %bitcast.5, s32[2,26]{1,0:T(2,128)} %bitcast.9, s32[1,1024]{1,0:T(1,128)} %order.1, bf16[27,256,256]{2,1,0:T(8,128)(2,1)} %refs_0_.1, bf16[256,768]{1,0:T(8,128)(2,1)} %refs_1_.1, ...), custom_call_target="tpu_custom_call" | custom-call | flops 20803747840 | bytes 6684672 | tf_op jit(solution)/shard_map/layer/pallas_call | solution.py:497
  70.4 2.1 %publish.1 = (bf16[1024,256]{1,0:T(8,128)(2,1)}, bf16[1024,256]{1,0:T(8,128)(2,1)}, f32[256,256]{1,0:T(8,128)}) custom-call(bf16[1024,256]{1,0:T(8,128)(2,1)} %get-tuple-element.9.refs_0_, bf16[1024,256]{1,0:T(8,128)(2,1)} %get-tuple-element.10.refs_1_, f32[256,256]{1,0:T(8,128)} %get-tuple-element.11.refs_2_), custom_call_target="tpu_custom_call" | custom-call | tf_op jit(solution)/shard_map/publish/pallas_call | solution.py:532
